TPU v7x, 128 devices: a whole 4x4x4 slice. The times are simulated.
128 devices in a mesh: node: 4 (over z), local: 16 (over x, y), tp: 2 (over core).
Axes of the slice: x: 4, y: 4, z: 4, core: 2. Of those that a mesh axis runs over, the one named last changes fastest.
Arguments:
- mixer_out: bfloat16 [8192, 8192], P(('node', 'local'), 'tp'), may hold values from -6 to 6
- out_proj: bfloat16 [8192, 8192], P('tp', 'local'), may hold values from -0.0625 to 0.0625
- residual: bfloat16 [8192, 8192], P(('node', 'tp'), 'local'), may hold values from -6 to 6
- norm_gain: float32 [8192], replicated, may hold values from 0.1 to 1.9
- router_weight: bfloat16 [8192, 16], replicated, may hold values from -0.0625 to 0.0625
- expert_ids: int32 [8192, 2], P(('node', 'tp')), may hold values from 0 to 15, as said below
- expert_gate: bfloat16 [4, 8192, 12288], P('node', None, ('local', 'tp')), may hold values from -0.0625 to 0.0625
- expert_up: bfloat16 [4, 8192, 12288], P('node', None, ('local', 'tp')), may hold values from -0.0625 to 0.0625
- expert_down: bfloat16 [4, 12288, 8192], P('node', ('local', 'tp')), may hold values from -0.4375 to 0.4375
Outputs:
- layer_out: bfloat16 [8192, 8192], P(('node', 'tp'), 'local')
Inputs may be any that keep to these rules, and one draw needn't show every extreme that they name: `expert_ids`: the ids of a row differ. A row names at most one of the experts 0 to 3, and only in its first column. In every aligned block of 1024 rows (the tokens of one (node, tp) group) each of these experts is named by at most 64 rows, and one of them, the same in every block of a draw, by exactly 64 rows.
All inputs are finite; a program needn't handle non-finite values.
Results may differ from a plain program's by a relative error of at most 0.009.
Values may be sent and summed in bfloat16 or wider, within the bound.
No kernel may reach another device: no remote copies, remote signals or barrier semaphores. Data moves between devices by JAX's collectives and lax.ppermute only.
A program may use at most 192 MiB of HBM per device.

v0:
```python
import jax
import jax.numpy as jnp
from jax import lax
from jax.sharding import PartitionSpec as P


def body(
    mixer_out,
    out_proj,
    residual,
    norm_gain,
    router_weight,
    expert_ids,
    expert_gate,
    expert_up,
    expert_down,
):
    node_count = lax.axis_size("node")
    local_count = lax.axis_size("local")
    tp_count = lax.axis_size("tp")
    group = local_count * tp_count
    half_rows = residual.shape[0]
    col_width = residual.shape[1]
    capacity = half_rows // 16
    partial_rows = jnp.dot(
        lax.all_gather(mixer_out, "local", axis=0, tiled=True),
        out_proj,
        preferred_element_type=jnp.float32,
    )
    mixed = lax.psum_scatter(partial_rows, "tp", scatter_dimension=0, tiled=True)
    stream = residual.astype(jnp.float32) + mixed
    stream_low = stream.astype(jnp.bfloat16)
    flights = jnp.arange(node_count, dtype=jnp.int32)
    chosen = jnp.any(expert_ids[:, :, None] == flights[None, None, :], axis=1)
    marks = chosen.astype(jnp.int32)
    slots = jnp.cumsum(marks, axis=0) - marks
    partner = jnp.where(expert_ids[:, 0] < node_count, expert_ids[:, 1], expert_ids[:, 0])
    places = jnp.arange(capacity, dtype=jnp.int32)
    picked = chosen.T[:, None, :] & (slots.T[:, None, :] == places[None, :, None])
    bucket = jnp.einsum(
        "nst,tc->nsc", picked.astype(jnp.bfloat16), stream_low, preferred_element_type=jnp.float32
    ).astype(jnp.bfloat16)
    bucket_ids = jnp.sum(jnp.where(picked, partner[None, None, :], 0), axis=2)
    spread = jnp.broadcast_to(bucket[:, None], (node_count, group, capacity, col_width)).reshape(
        node_count * group, capacity, col_width
    )
    spread_ids = jnp.broadcast_to(bucket_ids[:, None], (node_count, group, capacity)).reshape(
        node_count * group, capacity
    )
    landed, landed_ids = (
        lax.all_to_all(spread, ("node", "local", "tp"), split_axis=0, concat_axis=0, tiled=True),
        lax.all_to_all(
            spread_ids, ("node", "local", "tp"), split_axis=0, concat_axis=0, tiled=True
        ),
    )
    pieces = landed.reshape(node_count, local_count, tp_count, capacity, col_width)
    full_rows = pieces.transpose(0, 2, 3, 1, 4).reshape(
        node_count * tp_count * capacity, local_count * col_width
    )
    partner_rows = landed_ids.reshape(node_count, local_count, tp_count, capacity)[:, 0].reshape(-1)
    values = full_rows.astype(jnp.float32)
    scale = lax.rsqrt(jnp.mean(values * values, axis=1, keepdims=True) + 1e-06)
    normed = (values * scale * norm_gain[None, :]).astype(jnp.bfloat16)
    logits = jnp.dot(normed, router_weight, preferred_element_type=jnp.float32)
    own_logit = lax.dynamic_slice_in_dim(logits, lax.axis_index("node"), 1, 1)
    other_logit = jnp.take_along_axis(logits, partner_rows[:, None], axis=1)
    weight = jax.nn.sigmoid(own_logit - other_logit)
    gate = jnp.dot(normed, expert_gate[0], preferred_element_type=jnp.float32)
    upper = jnp.dot(normed, expert_up[0], preferred_element_type=jnp.float32)
    hidden = (jax.nn.silu(gate) * upper).astype(jnp.bfloat16)
    term = weight * jnp.dot(hidden, expert_down[0], preferred_element_type=jnp.float32)
    shaped = term.reshape(node_count, tp_count, capacity, local_count, col_width)
    outgoing = (
        shaped.transpose(0, 3, 1, 2, 4)
        .reshape(node_count * group, capacity, col_width)
        .astype(jnp.bfloat16)
    )
    incoming = lax.all_to_all(
        outgoing, ("node", "local", "tp"), split_axis=0, concat_axis=0, tiled=True
    )
    returned = jnp.sum(
        incoming.astype(jnp.float32).reshape(node_count, group, capacity, col_width), axis=1
    )
    safe_slots = jnp.clip(slots, 0, capacity - 1)
    fetched = returned[flights[None, :], safe_slots]
    expert_sum = jnp.sum(jnp.where(chosen[:, :, None], fetched, jnp.float32(0.0)), axis=1)
    return (stream + expert_sum).astype(jnp.bfloat16)


def solution(mesh):
    placed = (
        P(("node", "local"), "tp"),
        P("tp", "local"),
        P(("node", "tp"), "local"),
        P(),
        P(),
        P(("node", "tp"), None),
        P("node", None, ("local", "tp")),
        P("node", None, ("local", "tp")),
        P("node", ("local", "tp"), None),
    )
    return jax.shard_map(
        body, mesh=mesh, in_specs=placed, out_specs=P(("node", "tp"), "local"), check_vma=False
    )
```

profile of v0, /device:TPU:6, one launch (start us, length us, event | category | flops | bytes accessed | tf_op | source)
XLA Modules:
  0.0 600.5 jit_solution(9688043241767586082)
XLA Ops:
  6.5 0.0 all-gather.2.cloned.1.call-start
  6.5 0.7 all-gather.2.cloned.1.call-update
  7.3 0.0 reduce-scatter.2.cloned.1.call-start
  7.3 115.7 %all-gather.2.cloned.1.call-done = bf16[2048,4096]{1,0:T(8,128)(2,1)} async-done(((bf16[128,4096]{1,0:T(8,128)(2,1)}), bf16[2048,4096]{1,0:T(8,128)(2,1)}) %all-gather.2.cloned.1.call-update) | async-done | bytes 16777232 | tf_op jit(solution)/shard_map/all_gather | solution.py:26
  123.0 14.8 %fusion.37 = f32[2048,512]{1,0:T(8,128)} fusion(bf16[2048,4096]{1,0:T(8,128)(2,1)} %all-gather.2.cloned.1.call-done, bf16[4096,512]{1,0:T(8,128)(2,1)} %param.10), kind=kOutput, calls=%fused_computation.62 | convolution fusion | flops 8589934592 | bytes 25165824 | tf_op jit(solution)/shard_map/dot_general | solution.py:25
  137.8 0.0 reduce-scatter.2.cloned.1.call-update
  137.9 1.1 reduce-window.6
  139.1 0.2 slice_reduce_fusion
  139.3 0.2 reduce-window.9
  139.5 0.1 add_bitcast_fusion
  139.6 0.3 select_reduce_fusion.1
  139.9 0.6 broadcast_in_dim.62
  140.5 7.9 %all-to-all-start.1 = ((s32[128,1,64]{2,1,0:T(1,128)}), s32[128,1,64]{2,1,0:T(1,128)S(1)}, u32[]{:S(2)}, u32[]{:S(2)}) async-start(s32[128,1,64]{2,1,0:T(1,128)} %bitcast.8), calls=%async_computation.2 | async-start | bytes 131072 | tf_op jit(solution)/shard_map/all_to_all | solution.py:52
  148.5 4.2 reduce-scatter.2.cloned.1.call-done
  152.7 2.1 convolution_convert_fusion
  154.8 1.9 all-to-all-done.1
  156.7 4.3 broadcast_in_dim.33
  160.9 8.2 %all-to-all-start = ((bf16[128,64,512]{2,1,0:T(8,128)(2,1)}), bf16[128,64,512]{2,1,0:T(8,128)(2,1)}, u32[]{:S(2)}, u32[]{:S(2)}) async-start(bf16[128,64,512]{2,1,0:T(8,128)(2,1)} %bitcast.92), calls=%async_computation.1 | async-start | bytes 16777216 | tf_op jit(solution)/shard_map/all_to_all | solution.py:51
  169.1 0.0 copy-done.3
  169.2 0.1 broadcast_in_dim_reshape_squeeze.6
  169.3 0.1 broadcast_in_dim_reshape_squeeze.5
  169.4 99.1 %all-to-all-done = bf16[128,64,512]{2,1,0:T(8,128)(2,1)} async-done(((bf16[128,64,512]{2,1,0:T(8,128)(2,1)}), bf16[128,64,512]{2,1,0:T(8,128)(2,1)}, u32[]{:S(2)}, u32[]{:S(2)}) %all-to-all-start) | async-done | bytes 8388640 | tf_op jit(solution)/shard_map/all_to_all | solution.py:51
  268.5 5.1 fusion
  273.6 0.1 rsqrt.13
  273.7 9.7 %fusion.4 = bf16[4,2,64,16,512]{4,2,1,3,0:T(8,128)(2,1)} fusion(f32[16,512]{1,0:T(8,128)S(1)} %mul.65, f32[4,2,64]{2,1,0:T(2,128)S(1)} %add_rsqrt_fusion, bf16[128,64,512]{2,1,0:T(8,128)(2,1)} %all-to-all-done), kind=kLoop, calls=%fused_computation.12 | loop fusion | flops 16777216 | bytes 16812032 | tf_op jit(solution)/shard_map/mul | solution.py:63
  283.4 11.9 %copy.39 = bf16[4,2,64,16,512]{4,3,2,1,0:T(8,128)(2,1)} copy(bf16[4,2,64,16,512]{4,2,1,3,0:T(8,128)(2,1)} %fusion.4) | data formatting | bytes 16777216 | tf_op jit(solution)/shard_map/mul | solution.py:63
  295.3 16.6 %copy.45 = bf16[64,8,16,512]{3,1,2,0:T(8,128)(2,1)} copy(bf16[64,8,16,512]{3,2,1,0:T(8,128)(2,1)} %bitcast.94) | data formatting | bytes 16777216
  311.9 11.6 %convert_bitcast_fusion = f32[4,2,64,16,512]{4,2,1,3,0:T(8,128)} fusion(bf16[128,64,512]{2,1,0:T(8,128)(2,1)} %all-to-all-done), kind=kLoop, calls=%fused_computation.4 | loop fusion | flops 4194304 | bytes 25165824 | tf_op jit(solution)/shard_map/convert_element_type | solution.py:61
  323.4 18.3 %copy.38 = f32[4,2,64,16,512]{4,3,2,1,0:T(8,128)} copy(f32[4,2,64,16,512]{4,2,1,3,0:T(8,128)} %convert_bitcast_fusion) | data formatting | bytes 33554432 | tf_op jit(solution)/shard_map/convert_element_type | solution.py:61
  341.7 18.9 %copy.44 = f32[64,8,16,512]{3,1,2,0:T(8,128)S(1)} copy(f32[64,8,16,512]{3,2,1,0:T(8,128)} %bitcast.90) | data formatting | bytes 33554432
  360.6 0.0 slice-done
  360.6 4.5 fusion.10
  365.2 7.3 %fusion.16 = bf16[512,384]{1,0:T(8,128)(2,1)S(1)} fusion(bf16[512,8192]{1,0:T(8,128)(2,1)S(1)} %bitcast.99, bf16[1,8192,384]{2,1,0:T(8,128)(2,1)} %param.16, f32[512,384]{1,0:T(8,128)S(1)} %fusion.10), kind=kOutput, calls=%fused_computation.25 | convolution fusion | flops 3222405120 | bytes 15859712 | tf_op jit(solution)/shard_map/dot_general | solution.py:69
  372.5 2.4 fusion.3
  375.0 4.6 gather_fusion.1
  379.6 9.7 %multiply_convert_fusion = bf16[512,8192]{1,0:T(8,128)(2,1)} fusion(bf16[512,384]{1,0:T(8,128)(2,1)S(1)} %fusion.16, f32[512]{0:T(512)S(1)} %bitcast.109, bf16[1,384,8192]{2,1,0:T(8,128)(2,1)} %param.17), kind=kOutput, calls=%fused_computation.9 | convolution fusion | flops 3229614080 | bytes 15075328 | tf_op jit(solution)/shard_map/dot_general | solution.py:71
  389.2 11.0 %copy.46 = bf16[64,8,16,512]{3,2,1,0:T(8,128)(2,1)} copy(bf16[64,8,16,512]{3,1,2,0:T(8,128)(2,1)} %bitcast.100) | data formatting | bytes 16777216
  400.2 11.4 %copy.40 = bf16[4,2,64,16,512]{4,2,1,3,0:T(8,128)(2,1)} copy(bf16[4,2,64,16,512]{4,3,2,1,0:T(8,128)(2,1)} %bitcast.95) | data formatting | bytes 16777216 | tf_op jit(solution)/shard_map/convert_element_type | solution.py:76
  411.6 8.6 %all-to-all-start.2 = ((bf16[128,64,512]{2,1,0:T(8,128)(2,1)}), bf16[128,64,512]{2,1,0:T(8,128)(2,1)}, u32[]{:S(2)}, u32[]{:S(2)}) async-start(bf16[128,64,512]{2,1,0:T(8,128)(2,1)} %bitcast.93), calls=%async_computation.3 | async-start | bytes 16777216 | tf_op jit(solution)/shard_map/all_to_all | solution.py:78
  420.2 0.3 copy.37
  420.5 0.2 copy.41
  420.8 0.3 reshape.226
  421.0 98.5 %all-to-all-done.2 = bf16[128,64,512]{2,1,0:T(8,128)(2,1)} async-done(((bf16[128,64,512]{2,1,0:T(8,128)(2,1)}), bf16[128,64,512]{2,1,0:T(8,128)(2,1)}, u32[]{:S(2)}, u32[]{:S(2)}) %all-to-all-start.2) | async-done | bytes 8388640 | tf_op jit(solution)/shard_map/all_to_all | solution.py:78
  519.5 4.8 convert_reduce_fusion
  524.3 49.4 %gather_fusion = f32[4096,512]{1,0:T(8,128)} fusion(f32[4,64,512]{2,1,0:T(8,128)S(1)} %convert_reduce_fusion, s32[4096]{0:T(1024)S(1)} %reshape.226), kind=kCustom, calls=%fused_computation | custom fusion | bytes 16809984 | tf_op jit(solution)/shard_map/gather | solution.py:85
  573.7 9.8 %reshape.229 = f32[1024,4,512]{2,1,0:T(4,128)} reshape(f32[4096,512]{1,0:T(8,128)} %gather_fusion) | data formatting | bytes 16777216 | tf_op jit(solution)/shard_map/gather | solution.py:85
  583.6 8.1 %select_reduce_fusion = f32[1024,512]{1,0:T(8,128)S(1)} fusion(f32[1024,4,512]{2,1,0:T(4,128)} %reshape.229, pred[1024,4]{1,0:T(8,128)(4,1)S(1)} %copy.37), kind=kLoop, calls=%fused_computation.13 | loop fusion | flops 3670016 | bytes 10489856 | tf_op jit(solution)/shard_map/reduce_sum | solution.py:86
  591.7 1.7 add_convert_fusion
  (33 shorter events, 0.2 us)
Async XLA Ops:
  6.5 366.0 %copy-start = (bf16[8192,16]{0,1:T(8,128)(2,1)S(1)}, bf16[8192,16]{0,1:T(8,128)(2,1)}, u32[]{:S(2)}) copy-start(bf16[8192,16]{0,1:T(8,128)(2,1)} %param.13) | copy-start | bytes 786436
  6.5 116.5 %all-gather.2.cloned.1.call-start = ((), (), s32[]{:S(2)}) async-start(), calls=%async_computation.4 | async-start | bytes 17825792 | tf_op jit(solution)/shard_map/all_gather | solution.py:26
  7.3 130.6 %copy-start.4 = (s32[1024,2]{0,1:T(2,128)S(1)}, s32[1024,2]{0,1:T(2,128)}, u32[]{:S(2)}) copy-start(s32[1024,2]{0,1:T(2,128)} %param.14) | copy-start | bytes 24580
  7.3 145.4 %copy-start.2 = (bf16[1024,512]{1,0:T(8,128)(2,1)S(1)}, bf16[1024,512]{1,0:T(8,128)(2,1)}, u32[]{:S(2)}) copy-start(bf16[1024,512]{1,0:T(8,128)(2,1)} %param.11) | copy-start | bytes 3145732
  7.3 145.4 %reduce-scatter.2.cloned.1.call-start = ((), (), s32[]{:S(2)}) async-start(), calls=%async_computation.5 | async-start | bytes 6291456 | tf_op jit(solution)/shard_map/reduce_scatter | solution.py:30
  140.5 16.1 %all-to-all-start.1 = ((s32[128,1,64]{2,1,0:T(1,128)}), s32[128,1,64]{2,1,0:T(1,128)S(1)}, u32[]{:S(2)}, u32[]{:S(2)}) async-start(s32[128,1,64]{2,1,0:T(1,128)} %bitcast.8), calls=%async_computation.2 | async-start | bytes 131072 | tf_op jit(solution)/shard_map/all_to_all | solution.py:52
  160.9 8.2 %copy-start.3 = (f32[8192]{0:T(1024)S(1)}, f32[8192]{0:T(1024)}, u32[]{:S(2)}) copy-start(f32[8192]{0:T(1024)} %param.12) | copy-start | bytes 98308
  160.9 107.6 %all-to-all-start = ((bf16[128,64,512]{2,1,0:T(8,128)(2,1)}), bf16[128,64,512]{2,1,0:T(8,128)(2,1)}, u32[]{:S(2)}, u32[]{:S(2)}) async-start(bf16[128,64,512]{2,1,0:T(8,128)(2,1)} %bitcast.92), calls=%async_computation.1 | async-start | bytes 16777216 | tf_op jit(solution)/shard_map/all_to_all | solution.py:51
  323.4 37.2 %slice-start = ((s8[8388608]{0:T(1024)(128)(4,1)}), s8[4194304]{0:T(1024)(128)(4,1)S(1)}, s32[]{:S(2)}) async-start(s8[8388608]{0:T(1024)(128)(4,1)} %bitcast.96), calls=%async_computation.6 | async-start | bytes 8388608
  323.4 37.2 %slice-start.2 = ((s8[6291456]{0:T(1024)(128)(4,1)}), s8[4194304]{0:T(1024)(128)(4,1)S(1)}, s32[]{:S(2)}) async-start(s8[6291456]{0:T(1024)(128)(4,1)} %bitcast.110), calls=%async_computation.8 | async-start | bytes 8388608
  341.7 18.9 %slice-start.1 = ((s8[8388608]{0:T(1024)(128)(4,1)}), s8[4194304]{0:T(1024)(128)(4,1)S(1)}, s32[]{:S(2)}) async-start(s8[8388608]{0:T(1024)(128)(4,1)} %bitcast.96), calls=%async_computation.7 | async-start | bytes 8388608
  341.7 18.9 %slice-start.3 = ((s8[6291456]{0:T(1024)(128)(4,1)}), s8[2097152]{0:T(1024)(128)(4,1)S(1)}, s32[]{:S(2)}) async-start(s8[6291456]{0:T(1024)(128)(4,1)} %bitcast.110), calls=%async_computation.9 | async-start | bytes 4194304
  411.6 107.9 %all-to-all-start.2 = ((bf16[128,64,512]{2,1,0:T(8,128)(2,1)}), bf16[128,64,512]{2,1,0:T(8,128)(2,1)}, u32[]{:S(2)}, u32[]{:S(2)}) async-start(bf16[128,64,512]{2,1,0:T(8,128)(2,1)} %bitcast.93), calls=%async_computation.3 | async-start | bytes 16777216 | tf_op jit(solution)/shard_map/all_to_all | solution.py:78
  583.6 8.2 %copy-start.1 = (f32[1024,512]{1,0:T(8,128)S(1)}, f32[1024,512]{1,0:T(8,128)}, u32[]{:S(2)}) copy-start(f32[1024,512]{1,0:T(8,128)} %reduce-scatter.2.cloned.1.call-done) | copy-start | bytes 6291460
Sparse Core Ops, SparseCore 0:
  9.5 113.4 all-gather.1
  138.0 14.6 reduce-scatter.1
where the time goes:
time: 607 us; the launch traced here: 600 us
  waiting for transfers between devices  320 us (53%)
  local copies, waits for them, and re-layouts  158 us (26%)
  other arithmetic  42.9 us (7%)
  matrix products  40.9 us (7%)
  starting transfers between devices  24.7 us (4%)
  between operations  14 us (2%)
    all_gather x1, waiting for transfers between devices, body(): lax.all_gather(mixer_out, 'local', axis=0, tiled=True)  116 us
    all_to_all x1, waiting for transfers between devices, body(): lax.all_to_all(spread, ('node', 'local', 'tp'), split_axis=0, concat_axis...  99.1 us
    all_to_all x1, waiting for transfers between devices, body(): lax.all_to_all(outgoing, ('node', 'local', 'tp'), split_axis=0, concat_ax...  98.5 us
    gather x2, local copies, waits for them, and re-layouts, body(): fetched = returned[flights[None, :], safe_slots]  59.2 us
    unnamed x23, local copies, waits for them, and re-layouts  46.5 us
    convert_element_type x1, local copies, waits for them, and re-layouts, body(): values = full_rows.astype(jnp.float32)  18.3 us
    dot_general x1, matrix products, body(): jnp.dot(lax.all_gather(mixer_out, 'local', axis=0, tiled=True), out_proj,...  14.8 us
  transfers between devices with their start and end apart: 5, of which 5 were waited for; matrix products, arithmetic and copies ran while one was open for 1% of the time, Pallas kernels for 0%

commit v1 on v0

v1 whole, which is shorter than its diff:
```python
import jax
import jax.numpy as jnp
from jax import lax
from jax.experimental import pallas as pl
from jax.experimental.pallas import tpu as pltpu
from jax.sharding import PartitionSpec as P

CHUNKS = 4
SIDE = 4


def shift_node(value, by):
    return lax.ppermute(value, "node", [(i, (i + by) % SIDE) for i in range(SIDE)])


def shift_local(value, dx, dy):
    pairs = [
        (x * SIDE + y, ((x + dx) % SIDE) * SIDE + (y + dy) % SIDE)
        for x in range(SIDE)
        for y in range(SIDE)
    ]
    return lax.ppermute(value, "local", pairs)


def swap_core(value):
    return lax.ppermute(value, "tp", [(0, 1), (1, 0)])


def expert_kernel(
    order,
    rows,
    gain,
    router,
    select,
    gate_a,
    gate_b,
    up_a,
    up_b,
    down_a0,
    down_b0,
    down_a1,
    down_b1,
    out,
    acc,
    logit_acc,
    square_acc,
    hidden,
    weight,
    *,
    first_steps,
    width,
    features,
):
    step = pl.program_id(0)
    row_count, block = rows.shape[1], rows.shape[2]

    @pl.when(step == 0)
    def _():
        acc[...] = jnp.zeros_like(acc)
        logit_acc[...] = jnp.zeros_like(logit_acc)
        square_acc[...] = jnp.zeros_like(square_acc)

    @pl.when(step < first_steps)
    def _():
        for part in range(rows.shape[0]):
            span = pl.ds(part * block, block)
            values = rows[part].astype(jnp.float32)
            squares = values * values
            for lane in range(0, block, 128):
                square_acc[...] += squares[:, lane : lane + 128]
            scaled = (values * gain[:, span]).astype(jnp.bfloat16)
            for at, ref in enumerate((gate_a, gate_b, up_a, up_b)):
                acc[at] += jnp.dot(scaled, ref[0, span, :], preferred_element_type=jnp.float32)
            logit_acc[...] += jnp.dot(
                scaled, router[span, :], preferred_element_type=jnp.float32
            )

    @pl.when(step == first_steps - 1)
    def _():
        mean = jnp.sum(square_acc[...], axis=1, keepdims=True) / features
        scale = lax.rsqrt(mean + 1e-06)
        gap = jnp.sum(logit_acc[...] * select[...], axis=1, keepdims=True) * scale
        weight[...] = jnp.broadcast_to(1.0 / (1.0 + jnp.exp(-gap)), weight.shape)
        for core in range(2):
            gate = acc[core] * scale
            upper = acc[2 + core] * scale
            hidden[core] = (gate / (1.0 + jnp.exp(-gate)) * upper).astype(jnp.bfloat16)

    @pl.when(step >= first_steps)
    def _():
        for part, (ref_a, ref_b) in enumerate(((down_a0, down_b0), (down_a1, down_b1))):
            term = jnp.dot(hidden[0], ref_a[0], preferred_element_type=jnp.float32)
            term += jnp.dot(hidden[1], ref_b[0], preferred_element_type=jnp.float32)
            out[part] = (term * weight[:, :1]).astype(jnp.bfloat16)


def run_experts(rows, gain, router, select, order, gate, gate_o, up, up_o, down, down_o):
    blocks, row_count, block = rows.shape
    features, width = gate.shape[1], gate.shape[2]
    per = 2
    first_steps = blocks // per
    grid = (2 * first_steps,)
    head = lambda i: jnp.minimum(i, first_steps - 1)
    tail = lambda i: jnp.maximum(i - first_steps, 0)
    wide = pl.BlockSpec((1, per * block, width), lambda i, order: (0, head(i), 0))

    def down_spec(part):
        return pl.BlockSpec(
            (1, width, block), lambda i, order: (0, 0, order[tail(i) * per + part])
        )

    return pl.pallas_call(
        lambda *refs: expert_kernel(
            *refs, first_steps=first_steps, width=width, features=features
        ),
        out_shape=jax.ShapeDtypeStruct((blocks, row_count, block), jnp.bfloat16),
        grid_spec=pltpu.PrefetchScalarGridSpec(
            num_scalar_prefetch=1,
            grid=grid,
            in_specs=[
                pl.BlockSpec((per, row_count, block), lambda i, order: (head(i), 0, 0)),
                pl.BlockSpec((1, per * block), lambda i, order: (0, head(i))),
                pl.BlockSpec((per * block, router.shape[1]), lambda i, order: (head(i), 0)),
                pl.BlockSpec((row_count, router.shape[1]), lambda i, order: (0, 0)),
                wide,
                wide,
                wide,
                wide,
                down_spec(0),
                down_spec(0),
                down_spec(1),
                down_spec(1),
            ],
            out_specs=pl.BlockSpec((per, row_count, block), lambda i, order: (tail(i), 0, 0)),
            scratch_shapes=[
                pltpu.VMEM((4, row_count, width), jnp.float32),
                pltpu.VMEM((row_count, router.shape[1]), jnp.float32),
                pltpu.VMEM((row_count, 128), jnp.float32),
                pltpu.VMEM((2, row_count, width), jnp.bfloat16),
                pltpu.VMEM((row_count, 128), jnp.float32),
            ],
        ),
        compiler_params=pltpu.CompilerParams(
            dimension_semantics=("arbitrary",), vmem_limit_bytes=40 * 1024 * 1024
        ),
        cost_estimate=pl.CostEstimate(
            flops=2 * row_count * features * width * 6,
            bytes_accessed=features * width * 12 + 4 * blocks * row_count * block,
            transcendentals=0,
        ),
    )(order, rows, gain, router, select, gate, gate_o, up, up_o, down, down_o, down, down_o)


def plane_sum(spread):
    rows = spread.shape[2]
    half = rows // 2
    f32 = jnp.float32
    low, high = spread[:, :, :half], spread[:, :, half:]
    low_in = [shift_local(low[d], d, 0) for d in (1, 3, 2)]
    high_in = [shift_local(high[:, d], 0, d) for d in (1, 3, 2)]
    low = sum((v.astype(f32) for v in low_in), low[0].astype(f32)).astype(jnp.bfloat16)
    high = sum((v.astype(f32) for v in high_in), high[:, 0].astype(f32)).astype(jnp.bfloat16)
    low_in = [shift_local(low[d], 0, d) for d in (1, 3, 2)]
    high_in = [shift_local(high[d], d, 0) for d in (1, 3, 2)]
    low = sum((v.astype(f32) for v in low_in), low[0].astype(f32)).astype(jnp.bfloat16)
    high = sum((v.astype(f32) for v in high_in), high[0].astype(f32)).astype(jnp.bfloat16)
    return jnp.concatenate([low, high], axis=0)


def body(
    mixer_out,
    out_proj,
    residual,
    norm_gain,
    router_weight,
    expert_ids,
    expert_gate,
    expert_up,
    expert_down,
):
    f32 = jnp.float32
    node = lax.axis_index("node")
    local = lax.axis_index("local")
    core = lax.axis_index("tp")
    half_rows, col_width = residual.shape
    capacity = half_rows // 16
    spots = SIDE * capacity
    gate_o, up_o, down_o = (swap_core(w) for w in (expert_gate, expert_up, expert_down))

    first, partner = expert_ids[:, 0], expert_ids[:, 1]
    routed = first < SIDE
    relative = lax.rem(first - node + SIDE, SIDE)
    marks = (routed[:, None] & (relative[:, None] == jnp.arange(SIDE)[None, :])).astype(jnp.int32)
    slots = jnp.sum((jnp.cumsum(marks, axis=0) - marks) * marks, axis=1)
    spot = jnp.where(routed, relative * capacity + slots, -1)
    picked = spot[None, :] == jnp.arange(spots)[:, None]
    placed = (spot[:, None] == jnp.arange(spots)[None, :]).astype(jnp.bfloat16)
    partners = jnp.sum(jnp.where(picked, partner[None, :], 0), axis=1).reshape(SIDE, capacity)
    partners = jnp.concatenate(
        [partners[0]] + [shift_node(partners[d], d) for d in range(1, SIDE)], axis=0
    )
    experts = jnp.arange(router_weight.shape[1])[None, :]
    select = (experts == node).astype(f32) - (experts == partners[:, None]).astype(f32)
    picked = picked.astype(jnp.bfloat16)

    rows = mixer_out.shape[0] // CHUNKS
    streams = []
    for j in range(CHUNKS):
        full = lax.all_gather(mixer_out[j * rows : (j + 1) * rows], "local", axis=0, tiled=True)
        half = full.shape[0] // 2
        theirs = lax.dynamic_slice_in_dim(full, (1 - core) * half, half, 0)
        mine = lax.dynamic_slice_in_dim(full, core * half, half, 0)
        sent = swap_core(jnp.dot(theirs, out_proj, preferred_element_type=f32))
        kept = jnp.dot(mine, out_proj, preferred_element_type=f32)
        part = residual.reshape(-1, CHUNKS, rows, col_width)[:, j].astype(f32)
        streams.append(part + (kept + sent).reshape(part.shape))
    stream = jnp.stack(streams, axis=1).reshape(half_rows, col_width)
    stream_low = stream.astype(jnp.bfloat16)
    bucket = (
        jnp.dot(picked, stream_low, preferred_element_type=f32)
        .astype(jnp.bfloat16)
        .reshape(SIDE, capacity, col_width)
    )
    landed = jnp.concatenate(
        [bucket[0]] + [shift_node(bucket[d], d) for d in range(1, SIDE)], axis=0
    )
    gathered = lax.all_gather(landed, "local", axis=0, tiled=False)
    x, y = local // SIDE, local % SIDE
    ahead = jnp.arange(SIDE)
    order = (
        ((x + ahead) % SIDE)[:, None] * SIDE + ((y + ahead) % SIDE)[None, :]
    ).reshape(-1).astype(jnp.int32)
    spread = run_experts(
        gathered,
        norm_gain[None, :],
        router_weight,
        select,
        order,
        expert_gate,
        gate_o,
        expert_up,
        up_o,
        expert_down,
        down_o,
    )
    summed = plane_sum(spread.reshape(SIDE, SIDE, spots, col_width))
    summed = summed.reshape(SIDE, capacity, col_width)
    returned = jnp.concatenate(
        [summed[0]] + [shift_node(summed[d], -d) for d in range(1, SIDE)], axis=0
    )
    expert_sum = jnp.dot(placed, returned, preferred_element_type=f32)
    return (stream + expert_sum).astype(jnp.bfloat16)


def solution(mesh):
    placed = (
        P(("node", "local"), "tp"),
        P("tp", "local"),
        P(("node", "tp"), "local"),
        P(),
        P(),
        P(("node", "tp"), None),
        P("node", None, ("local", "tp")),
        P("node", None, ("local", "tp")),
        P("node", ("local", "tp"), None),
    )
    return jax.shard_map(
        body, mesh=mesh, in_specs=placed, out_specs=P(("node", "tp"), "local"), check_vma=False
    )
```

time: 607 us -> 394 us (0.65)
  local copies, waits for them, and re-layouts: 158 us -> 9.09 us
  other arithmetic: 42.9 us -> 5.66 us
  waiting for transfers between devices: 320 us -> 288 us
  Pallas kernels: 0 us -> 25 us
  matrix products: 40.9 us -> 25.1 us
    all_to_all x3 -> x0, waiting for transfers between devices: 199 us -> none  [the longest x1 99.1 us: body(): lax.all_to_all(spread, ('node', 'local', 'tp'), split_axis=0, concat_axis...]
    all_gather x1 -> x5, waiting for transfers between devices: 116 us -> 217 us  [the longest x4 196 us: body(): lax.all_gather(mixer_out[j * rows:(j + 1) * rows], 'local', axis=0, tiled...]
    ppermute x0 -> x28, waiting for transfers between devices: none -> 69.2 us  [the longest x12 33.9 us: shift_local(): return lax.ppermute(value, 'local', pairs)]
    gather x3 -> x0, local copies, waits for them, and re-layouts: 63.8 us -> none  [the longest x2 59.2 us: body(): fetched = returned[flights[None, :], safe_slots]]
    unnamed x23, local copies, waits for them, and re-layouts: 46.5 us -> 5.94 us
    convert_element_type x2 -> x0, local copies, waits for them, and re-layouts: 29.6 us -> none  [the longest x1 18.3 us: body(): values = full_rows.astype(jnp.float32)]
    ppermute x0 -> x28, starting transfers between devices: none -> 27.1 us  [the longest x12 13.3 us: shift_local(): return lax.ppermute(value, 'local', pairs)]
    pallas_call x0 -> x1, Pallas kernels: none -> 25 us  [run_experts(): pl.pallas_call(lambda *refs: expert_kernel(*refs, first_steps=first_steps...]
  transfers between devices with their start and end apart: 5 -> 33, of which waited for: 5 -> 22; matrix products, arithmetic and copies ran while one was open for 1% -> 7% of each run, Pallas kernels for 0% -> 0%
where the time goes in v1:
time: 394 us; the launch traced here: 393 us
  waiting for transfers between devices  288 us (73%)
  starting transfers between devices  27.2 us (7%)
  matrix products  25.1 us (6%)
  Pallas kernels  25 us (6%)
  between operations  13.6 us (3%)
  local copies, waits for them, and re-layouts  9.09 us (2%)
  other arithmetic  5.66 us (1%)
    all_gather x4, waiting for transfers between devices, body(): lax.all_gather(mixer_out[j * rows:(j + 1) * rows], 'local', axis=0, tiled...  196 us
    ppermute x12, waiting for transfers between devices, shift_local(): return lax.ppermute(value, 'local', pairs)  33.9 us
    pallas_call x1, Pallas kernels, run_experts(): pl.pallas_call(lambda *refs: expert_kernel(*refs, first_steps=first_steps...  25 us
    all_gather x1, waiting for transfers between devices, body(): gathered = lax.all_gather(landed, 'local', axis=0, tiled=False)  20.3 us
    ppermute x7, waiting for transfers between devices, swap_core(): return lax.ppermute(value, 'tp', [(0, 1), (1, 0)])  19.1 us
    dot_general x4, matrix products, body(): sent = swap_core(jnp.dot(theirs, out_proj, preferred_element_type=f32))  16.4 us
    ppermute x9, waiting for transfers between devices, shift_node(): lax.ppermute(value, 'node', [(i, (i + by) % SIDE) for i in range(SIDE)])  16.2 us
    ppermute x12, starting transfers between devices, shift_local(): return lax.ppermute(value, 'local', pairs)  13.3 us
  transfers between devices with their start and end apart: 33, of which 22 were waited for; matrix products, arithmetic and copies ran while one was open for 7% of the time, Pallas kernels for 0%

profile of v1, /device:TPU:6, one launch (start us, length us, event | category | flops | bytes accessed | tf_op | source)
XLA Modules:
  0.0 393.4 jit_solution(3025459974726857537)
XLA Ops:
  6.5 2.2 fusion.73
  12.4 1.1 reduce-window.6
  14.1 49.2 %all-gather.7.cloned.1.call-done = bf16[512,4096]{1,0:T(8,128)(2,1)} async-done(((bf16[32,4096]{1,0:T(8,128)(2,1)}), bf16[512,4096]{1,0:T(8,128)(2,1)}) %all-gather.7.cloned.1.call-update) | async-done | bytes 4194320 | tf_op jit(solution)/shard_map/all_gather | solution.py:209
  63.2 4.1 %fusion.13 = f32[256,512]{1,0:T(8,128)S(1)} fusion(bf16[4096,512]{1,0:T(8,128)(2,1)} %param.10, bf16[512,4096]{1,0:T(8,128)(2,1)} %all-gather.7.cloned.1.call-done, s32[]{:T(128)S(6)} %select_n.57), kind=kOutput, calls=%fused_computation.16 | convolution fusion | flops 1073741824 | bytes 6815748 | tf_op jit(solution)/shard_map/dot_general | solution.py:213
  67.4 49.1 %all-gather.9.cloned.1.call-done = bf16[512,4096]{1,0:T(8,128)(2,1)} async-done(((bf16[32,4096]{1,0:T(8,128)(2,1)}), bf16[512,4096]{1,0:T(8,128)(2,1)}) %all-gather.9.cloned.1.call-update) | async-done | bytes 4194320 | tf_op jit(solution)/shard_map/all_gather | solution.py:209
  116.5 4.1 %fusion.9 = f32[256,512]{1,0:T(8,128)S(1)} fusion(bf16[4096,512]{1,0:T(8,128)(2,1)} %param.10, bf16[512,4096]{1,0:T(8,128)(2,1)} %all-gather.9.cloned.1.call-done, s32[]{:T(128)S(6)} %select_n.57), kind=kOutput, calls=%fused_computation.12 | convolution fusion | flops 1073741824 | bytes 6815748 | tf_op jit(solution)/shard_map/dot_general | solution.py:213
  120.7 49.1 %all-gather.13.cloned.1.call-done = bf16[512,4096]{1,0:T(8,128)(2,1)} async-done(((bf16[32,4096]{1,0:T(8,128)(2,1)}), bf16[512,4096]{1,0:T(8,128)(2,1)}) %all-gather.13.cloned.1.call-update) | async-done | bytes 4194320 | tf_op jit(solution)/shard_map/all_gather | solution.py:209
  169.8 4.1 %fusion.1 = f32[256,512]{1,0:T(8,128)S(1)} fusion(bf16[4096,512]{1,0:T(8,128)(2,1)} %param.10, bf16[512,4096]{1,0:T(8,128)(2,1)} %all-gather.13.cloned.1.call-done, s32[]{:T(128)S(6)} %select_n.57), kind=kOutput, calls=%fused_computation.4 | convolution fusion | flops 1073741824 | bytes 6815748 | tf_op jit(solution)/shard_map/dot_general | solution.py:213
  174.0 49.0 %all-gather.11.cloned.1.call-done = bf16[512,4096]{1,0:T(8,128)(2,1)} async-done(((bf16[32,4096]{1,0:T(8,128)(2,1)}), bf16[512,4096]{1,0:T(8,128)(2,1)}) %all-gather.11.cloned.1.call-update) | async-done | bytes 4194320 | tf_op jit(solution)/shard_map/all_gather | solution.py:209
  223.0 4.2 %fusion.5 = f32[256,512]{1,0:T(8,128)S(1)} fusion(bf16[4096,512]{1,0:T(8,128)(2,1)} %param.10, bf16[512,4096]{1,0:T(8,128)(2,1)} %all-gather.11.cloned.1.call-done, s32[]{:T(128)S(6)} %select_n.57), kind=kOutput, calls=%fused_computation.8 | convolution fusion | flops 1073741824 | bytes 6815748 | tf_op jit(solution)/shard_map/dot_general | solution.py:213
  227.3 3.0 fusion.17
  230.4 1.2 fusion.20
  231.7 0.9 copy-done.9
  232.5 1.2 fusion.26
  234.0 1.2 fusion.23
  236.3 1.4 copy-done.2
  238.3 3.0 collective-permute-start.6
  241.9 1.0 collective-permute-start.4
  242.9 2.0 collective-permute-done.6
  244.9 2.7 collective-permute-done.5
  247.7 0.9 collective-permute-done.4
  251.6 2.2 collective-permute-done.9
  254.0 1.2 copy.43.refs_3_
  255.9 2.7 collective-permute-done.7
  258.8 1.1 collective-permute-done.10.refs_6_
  259.9 9.0 %collective-permute-done.11.refs_8_ = bf16[1,8192,384]{2,1,0:T(8,128)(2,1)} collective-permute-done((bf16[1,8192,384]{2,1,0:T(8,128)(2,1)}, bf16[1,8192,384]{2,1,0:T(8,128)(2,1)}, u32[]{:S(2)}, u32[]{:S(2)}) %collective-permute-start.11) | collective-permute-done | bytes 6291488 | tf_op jit(solution)/shard_map/ppermute | solution.py:26
  268.9 9.0 %collective-permute-done.12.refs_10_.refs_12_ = bf16[1,384,8192]{2,1,0:T(8,128)(2,1)} collective-permute-done((bf16[1,384,8192]{2,1,0:T(8,128)(2,1)}, bf16[1,384,8192]{2,1,0:T(8,128)(2,1)}, u32[]{:S(2)}, u32[]{:S(2)}) %collective-permute-start.12) | collective-permute-done | bytes 6291488 | tf_op jit(solution)/shard_map/ppermute | solution.py:26
  277.9 20.3 %all-gather.15.cloned.1.call-done = bf16[4096,512]{1,0:T(8,128)(2,1)} async-done(((bf16[256,512]{1,0:T(8,128)(2,1)}), bf16[4096,512]{1,0:T(8,128)(2,1)}) %all-gather.15.cloned.1.call-update) | async-done | bytes 4194320 | tf_op jit(solution)/shard_map/all_gather | solution.py:227
  298.2 2.2 copy-done
  300.4 25.0 %shard_map.91 = bf16[16,256,512]{2,1,0:T(8,128)(2,1)S(1)} custom-call(s32[16]{0:T(128)S(1)} %add.183.refs_0_, bf16[16,256,512]{2,1,0:T(8,128)(2,1)S(1)} %bitcast.117, f32[1,8192]{1,0:T(1,128)S(1)} %bitcast.118, bf16[8192,16]{1,0:T(8,128)(2,1)S(1)} %copy.43.refs_3_, f32[256,16]{1,0:T(8,128)S(1)} %convert_subtract_fusion.refs_4_, ...), custom_call_target="tpu_custom_call" | custom-call | flops 9663676416 | bytes 46137344 | tf_op jit(solution)/shard_map/pallas_call | solution.py:112
  325.8 2.1 collective-permute-start.22
  328.0 1.7 collective-permute-start.21
  329.8 2.2 collective-permute-start.13
  332.8 18.9 %collective-permute-done.20 = bf16[4,128,512]{2,1,0:T(8,128)(2,1)S(1)} collective-permute-done((bf16[4,128,512]{2,1,0:T(8,128)(2,1)S(1)}, bf16[4,128,512]{2,1,0:T(8,128)(2,1)S(1)}, u32[]{:S(2)}, u32[]{:S(2)}) %collective-permute-start.20) | collective-permute-done | bytes 524320 | tf_op jit(solution)/shard_map/ppermute | solution.py:22
  351.7 0.9 collective-permute-start.14
  352.7 0.9 collective-permute-done.13
  353.6 8.5 %collective-permute-done.14 = bf16[4,128,512]{2,1,0:T(8,128)(2,1)S(1)} collective-permute-done((bf16[4,128,512]{2,1,0:T(8,128)(2,1)S(1)}, bf16[4,128,512]{2,1,0:T(8,128)(2,1)S(1)}, u32[]{:S(2)}, u32[]{:S(2)}) %collective-permute-start.14) | collective-permute-done | bytes 524320 | tf_op jit(solution)/shard_map/ppermute | solution.py:22
  362.9 1.0 collective-permute-start.18
  363.9 2.2 collective-permute-start.17
  366.2 1.8 collective-permute-start.25
  368.0 2.4 collective-permute-done.16
  370.5 0.9 collective-permute-done.17
  371.4 3.0 collective-permute-start.19
  374.5 2.2 collective-permute-done.24
  376.7 3.2 collective-permute-start.26
  380.6 1.9 collective-permute-done.26
  382.6 2.9 collective-permute-done.27
  385.4 1.5 fusion
  (91 shorter events, 13.9 us)
Async XLA Ops:
  6.5 56.7 %all-gather.7.cloned.1.call-start = ((), (), s32[]{:S(2)}) async-start(), calls=%async_computation | async-start | bytes 4456448 | tf_op jit(solution)/shard_map/all_gather | solution.py:209
  8.7 107.8 %all-gather.9.cloned.1.call-start = ((), (), s32[]{:S(2)}) async-start(), calls=%async_computation.1 | async-start | bytes 4456448 | tf_op jit(solution)/shard_map/all_gather | solution.py:209
  9.5 160.3 %all-gather.13.cloned.1.call-start = ((), (), s32[]{:S(2)}) async-start(), calls=%async_computation.3 | async-start | bytes 4456448 | tf_op jit(solution)/shard_map/all_gather | solution.py:209
  10.2 212.7 %all-gather.11.cloned.1.call-start = ((), (), s32[]{:S(2)}) async-start(), calls=%async_computation.2 | async-start | bytes 4456448 | tf_op jit(solution)/shard_map/all_gather | solution.py:209
  10.8 287.4 %all-gather.15.cloned.1.call-start = ((), (), s32[]{:S(2)}) async-start(), calls=%async_computation.4 | async-start | bytes 4456448 | tf_op jit(solution)/shard_map/all_gather | solution.py:227
  67.3 160.0 %collective-permute-start = (f32[256,512]{1,0:T(8,128)S(1)}, f32[256,512]{1,0:T(8,128)S(1)}, u32[]{:S(2)}, u32[]{:S(2)}) collective-permute-start(f32[256,512]{1,0:T(8,128)S(1)} %fusion.13), channel_id=1, source_target_pairs={{0,1},{1,0},{2,3},{3,2},{4,5},{5,4},{6,7},{7,6},{8,9},{9,8},{10,11... | collective-permute-start | bytes 1572872 | tf_op jit(solution)/shard_map/ppermute | solution.py:26
  120.6 109.8 %collective-permute-start.1 = (f32[256,512]{1,0:T(8,128)S(1)}, f32[256,512]{1,0:T(8,128)S(1)}, u32[]{:S(2)}, u32[]{:S(2)}) collective-permute-start(f32[256,512]{1,0:T(8,128)S(1)} %fusion.9), channel_id=1, source_target_pairs={{0,1},{1,0},{2,3},{3,2},{4,5},{5,4},{6,7},{7,6},{8,9},{9,8},{10,11... | collective-permute-start | bytes 1572872 | tf_op jit(solution)/shard_map/ppermute | solution.py:26
  173.9 57.8 %collective-permute-start.3 = (f32[256,512]{1,0:T(8,128)S(1)}, f32[256,512]{1,0:T(8,128)S(1)}, u32[]{:S(2)}, u32[]{:S(2)}) collective-permute-start(f32[256,512]{1,0:T(8,128)S(1)} %fusion.1), channel_id=1, source_target_pairs={{0,1},{1,0},{2,3},{3,2},{4,5},{5,4},{6,7},{7,6},{8,9},{9,8},{10,11... | collective-permute-start | bytes 1572872 | tf_op jit(solution)/shard_map/ppermute | solution.py:26
  223.0 4.3 %copy-start.7 = (bf16[4096,512]{1,0:T(8,128)(2,1)S(1)}, bf16[4096,512]{1,0:T(8,128)(2,1)}, u32[]{:S(2)}) copy-start(bf16[4096,512]{1,0:T(8,128)(2,1)} %param.10) | copy-start | bytes 12582916
  227.2 3.2 copy-start.8
  227.2 6.6 %collective-permute-start.2 = (f32[256,512]{1,0:T(8,128)S(1)}, f32[256,512]{1,0:T(8,128)S(1)}, u32[]{:S(2)}, u32[]{:S(2)}) collective-permute-start(f32[256,512]{1,0:T(8,128)S(1)} %fusion.5), channel_id=1, source_target_pairs={{0,1},{1,0},{2,3},{3,2},{4,5},{5,4},{6,7},{7,6},{8,9},{9,8},{10,11... | collective-permute-start | bytes 1572872 | tf_op jit(solution)/shard_map/ppermute | solution.py:26
  230.4 2.2 copy-start.9
  231.6 2.4 copy-start.10
  233.8 1.5 copy-start.4
  236.0 18.0 %copy-start.5 = (bf16[8192,16]{0,1:T(8,128)(2,1)S(1)}, bf16[8192,16]{0,1:T(8,128)(2,1)}, u32[]{:S(2)}) copy-start(bf16[8192,16]{0,1:T(8,128)(2,1)} %param.13) | copy-start | bytes 786436
  236.3 1.4 copy-start.2
  237.7 60.6 %copy-start.1 = (f32[8192]{0:T(1024)S(1)}, f32[8192]{0:T(1024)}, u32[]{:S(2)}) copy-start(f32[8192]{0:T(1024)} %param.12) | copy-start | bytes 98308
  238.3 6.7 %collective-permute-start.6 = (bf16[64,512]{1,0:T(8,128)(2,1)S(1)}, bf16[64,512]{1,0:T(8,128)(2,1)S(1)}, u32[]{:S(2)}, u32[]{:S(2)}) collective-permute-start(bf16[64,512]{1,0:T(8,128)(2,1)S(1)} %get-tuple-element.30), channel_id=1, source_target_pairs={{0,96},{32,0},{64,32},{96,64},{1,97},{33,1},{65,33},{97,65},{2,98}... | collective-permute-start | bytes 196616 | tf_op jit(solution)/shard_map/ppermute | solution.py:13
  241.3 6.4 %collective-permute-start.5 = (bf16[64,512]{1,0:T(8,128)(2,1)S(1)}, bf16[64,512]{1,0:T(8,128)(2,1)S(1)}, u32[]{:S(2)}, u32[]{:S(2)}) collective-permute-start(bf16[64,512]{1,0:T(8,128)(2,1)S(1)} %get-tuple-element.31), channel_id=1, source_target_pairs={{0,64},{32,96},{64,0},{96,32},{1,65},{33,97},{65,1},{97,33},{2,66}... | collective-permute-start | bytes 196616 | tf_op jit(solution)/shard_map/ppermute | solution.py:13
  241.9 6.7 %collective-permute-start.4 = (bf16[64,512]{1,0:T(8,128)(2,1)S(1)}, bf16[64,512]{1,0:T(8,128)(2,1)S(1)}, u32[]{:S(2)}, u32[]{:S(2)}) collective-permute-start(bf16[64,512]{1,0:T(8,128)(2,1)S(1)} %get-tuple-element.32), channel_id=1, source_target_pairs={{0,32},{32,64},{64,96},{96,0},{1,33},{33,65},{65,97},{97,1},{2,34}... | collective-permute-start | bytes 196616 | tf_op jit(solution)/shard_map/ppermute | solution.py:13
  249.4 10.6 %collective-permute-start.10 = (bf16[1,8192,384]{2,1,0:T(8,128)(2,1)}, bf16[1,8192,384]{2,1,0:T(8,128)(2,1)}, u32[]{:S(2)}, u32[]{:S(2)}) collective-permute-start(bf16[1,8192,384]{2,1,0:T(8,128)(2,1)} %refs_5_.1), channel_id=1, source_target_pairs={{0,1},{1,0},{2,3},{3,2},{4,5},{5,4},{6,7},{7,6},{8,9},{9,8},{10,11... | collective-permute-start | bytes 18874376 | tf_op jit(solution)/shard_map/ppermute | solution.py:26
  249.5 19.5 %collective-permute-start.11 = (bf16[1,8192,384]{2,1,0:T(8,128)(2,1)}, bf16[1,8192,384]{2,1,0:T(8,128)(2,1)}, u32[]{:S(2)}, u32[]{:S(2)}) collective-permute-start(bf16[1,8192,384]{2,1,0:T(8,128)(2,1)} %refs_7_.1), channel_id=1, source_target_pairs={{0,1},{1,0},{2,3},{3,2},{4,5},{5,4},{6,7},{7,6},{8,9},{9,8},{10,11... | collective-permute-start | bytes 18874376 | tf_op jit(solution)/shard_map/ppermute | solution.py:26
  250.0 28.0 %collective-permute-start.12 = (bf16[1,384,8192]{2,1,0:T(8,128)(2,1)}, bf16[1,384,8192]{2,1,0:T(8,128)(2,1)}, u32[]{:S(2)}, u32[]{:S(2)}) collective-permute-start(bf16[1,384,8192]{2,1,0:T(8,128)(2,1)} %refs_11_.1), channel_id=1, source_target_pairs={{0,1},{1,0},{2,3},{3,2},{4,5},{5,4},{6,7},{7,6},{8,9},{9,8},{10,11... | collective-permute-start | bytes 18874376 | tf_op jit(solution)/shard_map/ppermute | solution.py:26
  250.3 3.5 collective-permute-start.9
  250.9 5.0 %collective-permute-start.8 = (s32[64]{0:T(128)S(1)}, s32[64]{0:T(128)S(1)}, u32[]{:S(2)}, u32[]{:S(2)}) collective-permute-start(s32[64]{0:T(128)S(1)} %get-tuple-element.40), channel_id=1, source_target_pairs={{0,64},{32,96},{64,0},{96,32},{1,65},{33,97},{65,1},{97,33},{2,66}... | collective-permute-start | bytes 776 | tf_op jit(solution)/shard_map/ppermute | solution.py:13
  253.9 4.8 %collective-permute-start.7 = (s32[64]{0:T(128)S(1)}, s32[64]{0:T(128)S(1)}, u32[]{:S(2)}, u32[]{:S(2)}) collective-permute-start(s32[64]{0:T(128)S(1)} %get-tuple-element.41), channel_id=1, source_target_pairs={{0,32},{32,64},{64,96},{96,0},{1,33},{33,65},{65,97},{97,1},{2,34}... | collective-permute-start | bytes 776 | tf_op jit(solution)/shard_map/ppermute | solution.py:13
  298.2 2.2 copy-start
  325.6 26.2 %collective-permute-start.20 = (bf16[4,128,512]{2,1,0:T(8,128)(2,1)S(1)}, bf16[4,128,512]{2,1,0:T(8,128)(2,1)S(1)}, u32[]{:S(2)}, u32[]{:S(2)}) collective-permute-start(bf16[4,128,512]{2,1,0:T(8,128)(2,1)S(1)} %get-tuple-element.12), channel_id=1, source_target_pairs={{0,2},{2,4},{4,6},{6,0},{8,10},{10,12},{12,14},{14,8},{16,18},{18,... | collective-permute-start | bytes 1572872 | tf_op jit(solution)/shard_map/ppermute | solution.py:22
  325.8 26.8 %collective-permute-start.22 = (bf16[4,128,512]{2,1,0:T(8,128)(2,1)S(1)}, bf16[4,128,512]{2,1,0:T(8,128)(2,1)S(1)}, u32[]{:S(2)}, u32[]{:S(2)}) collective-permute-start(bf16[4,128,512]{2,1,0:T(8,128)(2,1)S(1)} %get-tuple-element.13), channel_id=1, source_target_pairs={{0,4},{2,6},{4,0},{6,2},{8,12},{10,14},{12,8},{14,10},{16,20},{18,... | collective-permute-start | bytes 1572872 | tf_op jit(solution)/shard_map/ppermute | solution.py:22
  328.0 24.7 %collective-permute-start.21 = (bf16[4,128,512]{2,1,0:T(8,128)(2,1)S(1)}, bf16[4,128,512]{2,1,0:T(8,128)(2,1)S(1)}, u32[]{:S(2)}, u32[]{:S(2)}) collective-permute-start(bf16[4,128,512]{2,1,0:T(8,128)(2,1)S(1)} %get-tuple-element.14), channel_id=1, source_target_pairs={{0,6},{2,0},{4,2},{6,4},{8,14},{10,8},{12,10},{14,12},{16,22},{18,... | collective-permute-start | bytes 1572872 | tf_op jit(solution)/shard_map/ppermute | solution.py:22
  329.8 23.8 %collective-permute-start.13 = (bf16[4,128,512]{2,1,0:T(8,128)(2,1)S(1)}, bf16[4,128,512]{2,1,0:T(8,128)(2,1)S(1)}, u32[]{:S(2)}, u32[]{:S(2)}) collective-permute-start(bf16[4,128,512]{2,1,0:T(8,128)(2,1)S(1)} %get-tuple-element.9), channel_id=1, source_target_pairs={{0,8},{2,10},{4,12},{6,14},{8,16},{10,18},{12,20},{14,22},{16,24},... | collective-permute-start | bytes 1572872 | tf_op jit(solution)/shard_map/ppermute | solution.py:22
  332.0 21.6 %collective-permute-start.15 = (bf16[4,128,512]{2,1,0:T(8,128)(2,1)S(1)}, bf16[4,128,512]{2,1,0:T(8,128)(2,1)S(1)}, u32[]{:S(2)}, u32[]{:S(2)}) collective-permute-start(bf16[4,128,512]{2,1,0:T(8,128)(2,1)S(1)} %get-tuple-element.10), channel_id=1, source_target_pairs={{0,16},{2,18},{4,20},{6,22},{8,24},{10,26},{12,28},{14,30},{16,0},... | collective-permute-start | bytes 1572872 | tf_op jit(solution)/shard_map/ppermute | solution.py:22
  351.7 28.9 %copy-start.6 = (s32[1024,2]{0,1:T(2,128)S(1)}, s32[1024,2]{0,1:T(2,128)}, u32[]{:S(2)}) copy-start(s32[1024,2]{0,1:T(2,128)} %param.14) | copy-start | bytes 24580
  351.7 33.7 %copy-start.3 = (f32[8,4,32,512]{3,2,1,0:T(8,128)S(1)}, f32[8,4,32,512]{3,2,1,0:T(8,128)}, u32[]{:S(2)}) copy-start(f32[8,4,32,512]{3,2,1,0:T(8,128)} %copy-done.2) | copy-start | bytes 6291460
  351.7 10.4 %collective-permute-start.14 = (bf16[4,128,512]{2,1,0:T(8,128)(2,1)S(1)}, bf16[4,128,512]{2,1,0:T(8,128)(2,1)S(1)}, u32[]{:S(2)}, u32[]{:S(2)}) collective-permute-start(bf16[4,128,512]{2,1,0:T(8,128)(2,1)S(1)} %get-tuple-element.11), channel_id=1, source_target_pairs={{0,24},{2,26},{4,28},{6,30},{8,0},{10,2},{12,4},{14,6},{16,8},{18,... | collective-permute-start | bytes 1572872 | tf_op jit(solution)/shard_map/ppermute | solution.py:22
  362.8 7.7 %collective-permute-start.16 = (bf16[128,512]{1,0:T(8,128)(2,1)S(1)}, bf16[128,512]{1,0:T(8,128)(2,1)S(1)}, u32[]{:S(2)}, u32[]{:S(2)}) collective-permute-start(bf16[128,512]{1,0:T(8,128)(2,1)S(1)} %get-tuple-element.23), channel_id=1, source_target_pairs={{0,2},{2,4},{4,6},{6,0},{8,10},{10,12},{12,14},{14,8},{16,18},{18,... | collective-permute-start | bytes 393224 | tf_op jit(solution)/shard_map/ppermute | solution.py:22
  362.9 7.6 %collective-permute-start.18 = (bf16[128,512]{1,0:T(8,128)(2,1)S(1)}, bf16[128,512]{1,0:T(8,128)(2,1)S(1)}, u32[]{:S(2)}, u32[]{:S(2)}) collective-permute-start(bf16[128,512]{1,0:T(8,128)(2,1)S(1)} %get-tuple-element.24), channel_id=1, source_target_pairs={{0,4},{2,6},{4,0},{6,2},{8,12},{10,14},{12,8},{14,10},{16,20},{18,... | collective-permute-start | bytes 393224 | tf_op jit(solution)/shard_map/ppermute | solution.py:22
  363.9 7.4 %collective-permute-start.17 = (bf16[128,512]{1,0:T(8,128)(2,1)S(1)}, bf16[128,512]{1,0:T(8,128)(2,1)S(1)}, u32[]{:S(2)}, u32[]{:S(2)}) collective-permute-start(bf16[128,512]{1,0:T(8,128)(2,1)S(1)} %get-tuple-element.25), channel_id=1, source_target_pairs={{0,6},{2,0},{4,2},{6,4},{8,14},{10,8},{12,10},{14,12},{16,22},{18,... | collective-permute-start | bytes 393224 | tf_op jit(solution)/shard_map/ppermute | solution.py:22
  366.1 8.3 %collective-permute-start.23 = (bf16[128,512]{1,0:T(8,128)(2,1)S(1)}, bf16[128,512]{1,0:T(8,128)(2,1)S(1)}, u32[]{:S(2)}, u32[]{:S(2)}) collective-permute-start(bf16[128,512]{1,0:T(8,128)(2,1)S(1)} %get-tuple-element.26), channel_id=1, source_target_pairs={{0,8},{2,10},{4,12},{6,14},{8,16},{10,18},{12,20},{14,22},{16,24},... | collective-permute-start | bytes 393224 | tf_op jit(solution)/shard_map/ppermute | solution.py:22
  366.2 8.2 %collective-permute-start.25 = (bf16[128,512]{1,0:T(8,128)(2,1)S(1)}, bf16[128,512]{1,0:T(8,128)(2,1)S(1)}, u32[]{:S(2)}, u32[]{:S(2)}) collective-permute-start(bf16[128,512]{1,0:T(8,128)(2,1)S(1)} %get-tuple-element.27), channel_id=1, source_target_pairs={{0,16},{2,18},{4,20},{6,22},{8,24},{10,26},{12,28},{14,30},{16,0},... | collective-permute-start | bytes 393224 | tf_op jit(solution)/shard_map/ppermute | solution.py:22
  370.4 6.2 %collective-permute-start.24 = (bf16[128,512]{1,0:T(8,128)(2,1)S(1)}, bf16[128,512]{1,0:T(8,128)(2,1)S(1)}, u32[]{:S(2)}, u32[]{:S(2)}) collective-permute-start(bf16[128,512]{1,0:T(8,128)(2,1)S(1)} %get-tuple-element.28), channel_id=1, source_target_pairs={{0,24},{2,26},{4,28},{6,30},{8,0},{10,2},{12,4},{14,6},{16,8},{18,... | collective-permute-start | bytes 393224 | tf_op jit(solution)/shard_map/ppermute | solution.py:22
  371.4 9.2 %collective-permute-start.19 = (bf16[64,512]{1,0:T(8,128)(2,1)S(1)}, bf16[64,512]{1,0:T(8,128)(2,1)S(1)}, u32[]{:S(2)}, u32[]{:S(2)}) collective-permute-start(bf16[64,512]{1,0:T(8,128)(2,1)S(1)} %get-tuple-element.34), channel_id=1, source_target_pairs={{0,96},{32,0},{64,32},{96,64},{1,97},{33,1},{65,33},{97,65},{2,98}... | collective-permute-start | bytes 196616 | tf_op jit(solution)/shard_map/ppermute | solution.py:13
  376.7 5.8 %collective-permute-start.26 = (bf16[64,512]{1,0:T(8,128)(2,1)S(1)}, bf16[64,512]{1,0:T(8,128)(2,1)S(1)}, u32[]{:S(2)}, u32[]{:S(2)}) collective-permute-start(bf16[64,512]{1,0:T(8,128)(2,1)S(1)} %get-tuple-element.35), channel_id=1, source_target_pairs={{0,64},{32,96},{64,0},{96,32},{1,65},{33,97},{65,1},{97,33},{2,66}... | collective-permute-start | bytes 196616 | tf_op jit(solution)/shard_map/ppermute | solution.py:13
  379.9 5.5 %collective-permute-start.27 = (bf16[64,512]{1,0:T(8,128)(2,1)S(1)}, bf16[64,512]{1,0:T(8,128)(2,1)S(1)}, u32[]{:S(2)}, u32[]{:S(2)}) collective-permute-start(bf16[64,512]{1,0:T(8,128)(2,1)S(1)} %get-tuple-element.36), channel_id=1, source_target_pairs={{0,32},{32,64},{64,96},{96,0},{1,33},{33,65},{65,97},{97,1},{2,34}... | collective-permute-start | bytes 196616 | tf_op jit(solution)/shard_map/ppermute | solution.py:13
Sparse Core Ops, SparseCore 0:
  9.5 53.7 all-gather.6
  65.4 51.0 all-gather.8
  118.7 51.0 all-gather.12
  171.8 51.0 all-gather.10
  249.5 48.6 all-gather.14

commit v2 on v0

v2 whole, which is shorter than its diff:
```python
import jax
import jax.numpy as jnp
from jax import lax
from jax.experimental import pallas as pl
from jax.experimental.pallas import tpu as pltpu
from jax.sharding import PartitionSpec as P

SIDE = 4
PER = 1
VMEM = 56 * 1024 * 1024
F32 = jnp.float32
BF16 = jnp.bfloat16


def shift_node(value, by):
    return lax.ppermute(value, "node", [(i, (i + by) % SIDE) for i in range(SIDE)])


def shift(value, axis, by):
    dx, dy = (by, 0) if axis == "x" else (0, by)
    pairs = [
        (x * SIDE + y, ((x + dx) % SIDE) * SIDE + (y + dy) % SIDE)
        for x in range(SIDE)
        for y in range(SIDE)
    ]
    return lax.ppermute(value, "local", pairs)


def shift_mixed(value, far, by):
    pairs = []
    for x in range(SIDE):
        for y in range(SIDE):
            for core in range(2):
                dx, dy = (by, 0) if (core == 0) != far else (0, by)
                to = ((x + dx) % SIDE) * SIDE + (y + dy) % SIDE
                pairs.append(((x * SIDE + y) * 2 + core, to * 2 + core))
    return lax.ppermute(value, ("local", "tp"), pairs)


def swap_core(value):
    return lax.ppermute(value, "tp", [(0, 1), (1, 0)])


def roll_to(value, by, axis):
    doubled = jnp.concatenate([value, value], axis=axis)
    return lax.dynamic_slice_in_dim(doubled, by, value.shape[axis], axis)


def ring(value, axis):
    half = value.shape[0] // 2
    behind = shift(value, axis, 1)
    ahead = shift(value, axis, -1)
    across = [shift(behind[:half], axis, 1), shift(ahead[half:], axis, -1)]
    return ahead, across, behind


def products_kernel(order, rows, *refs, first, last, features):
    weights, refs = [refs[2 * b : 2 * b + 2] for b in range(PER)], refs[2 * PER :]
    routers, refs = refs[:PER], refs[PER:]
    gains, refs = refs[:PER], refs[PER:]
    carried = None
    if not first:
        carried, refs = refs[:3], refs[3:]
    if last:
        select, hidden, weight, acc, logits, squares = refs
    else:
        acc, logits, squares = refs

    @pl.when(pl.program_id(0) == 0)
    def _():
        for at, ref in enumerate((acc, logits, squares)):
            ref[...] = jnp.zeros_like(ref) if first else carried[at][...]

    scaled = []
    for b in range(PER):
        values = rows[b].astype(F32)
        square = values * values
        for lane in range(0, values.shape[1], 128):
            squares[...] += square[:, lane : lane + 128]
        scaled.append((values * gains[b][...]).astype(BF16))
    for at in range(2):
        for core in range(2):
            total = acc[2 * at + core]
            for b in range(PER):
                total += jnp.dot(scaled[b], weights[b][at][core], preferred_element_type=F32)
            acc[2 * at + core] = total
    total = logits[...]
    for b in range(PER):
        total += lax.dot_general(
            scaled[b], routers[b][...], (((1,), (1,)), ((), ())), preferred_element_type=F32
        )
    logits[...] = total

    if last:

        @pl.when(pl.program_id(0) == pl.num_programs(0) - 1)
        def _():
            mean = jnp.sum(squares[...], axis=1, keepdims=True) / features
            scale = lax.rsqrt(mean + 1e-06)
            gap = jnp.sum(logits[...] * select[...], axis=1, keepdims=True) * scale
            weight[...] = jnp.broadcast_to(1.0 / (1.0 + jnp.exp(-gap)), weight.shape)
            for core in range(2):
                gate = acc[core] * scale
                upper = acc[2 + core] * scale
                width = gate.shape[1]
                hidden[:, core * width : (core + 1) * width] = (
                    gate / (1.0 + jnp.exp(-gate)) * upper
                ).astype(BF16)


def products(rows, places, gate, up, router, gain, carried, select):
    blocks, count, depth = rows.shape
    features, width = gate.shape[1:]
    experts = router.shape[0]
    first, last = carried is None, select is not None
    whole = lambda *shape: pl.BlockSpec(shape, lambda i, order: (0,) * len(shape))

    def weight_spec(b):
        return pl.BlockSpec((2, depth, width), lambda i, order: (0, order[i * PER + b], 0))

    def flat_spec(b, height):
        return pl.BlockSpec((height, depth), lambda i, order: (0, order[i * PER + b]))

    in_specs = [pl.BlockSpec((PER, count, depth), lambda i, order: (i, 0, 0))]
    operands = [rows]
    for b in range(PER):
        in_specs += [weight_spec(b)] * 2
        operands += [gate, up]
    in_specs += [flat_spec(b, experts) for b in range(PER)]
    operands += [router] * PER
    in_specs += [flat_spec(b, 1) for b in range(PER)]
    operands += [gain] * PER
    sums = [(4, count, width), (count, experts), (count, 128)]
    if not first:
        in_specs += [whole(*shape) for shape in sums]
        operands += list(carried)
    scratch = []
    if last:
        in_specs.append(whole(count, experts))
        operands.append(select)
        out_shape = [
            jax.ShapeDtypeStruct((count, 2 * width), BF16),
            jax.ShapeDtypeStruct((count, 128), F32),
        ]
        scratch = [pltpu.VMEM(shape, F32) for shape in sums]
    else:
        out_shape = [jax.ShapeDtypeStruct(shape, F32) for shape in sums]
    return pl.pallas_call(
        lambda *refs: products_kernel(*refs, first=first, last=last, features=features),
        out_shape=out_shape,
        grid_spec=pltpu.PrefetchScalarGridSpec(
            num_scalar_prefetch=1,
            grid=(blocks // PER,),
            in_specs=in_specs,
            out_specs=[whole(*s.shape) for s in out_shape],
            scratch_shapes=scratch,
        ),
        compiler_params=pltpu.CompilerParams(
            dimension_semantics=("arbitrary",), vmem_limit_bytes=VMEM
        ),
        cost_estimate=pl.CostEstimate(
            flops=2 * count * depth * blocks * width * 4,
            bytes_accessed=blocks * depth * width * 8,
            transcendentals=0,
        ),
    )(places, *operands)


def down_kernel(order, hidden, weight, *refs):
    *downs, out = refs
    width = hidden.shape[1] // 2
    for b, ref in enumerate(downs):
        term = jnp.dot(hidden[:, :width], ref[0], preferred_element_type=F32)
        term += jnp.dot(hidden[:, width:], ref[1], preferred_element_type=F32)
        out[b] = (term * weight[:, :1]).astype(BF16)


def down_terms(hidden, weight, places, down, depth):
    count, both = hidden.shape
    blocks = places.shape[0]
    whole = lambda *shape: pl.BlockSpec(shape, lambda i, order: (0,) * len(shape))

    def down_spec(b):
        return pl.BlockSpec(
            (2, both // 2, depth), lambda i, order: (0, 0, order[i * PER + b])
        )

    return pl.pallas_call(
        down_kernel,
        out_shape=jax.ShapeDtypeStruct((blocks, count, depth), BF16),
        grid_spec=pltpu.PrefetchScalarGridSpec(
            num_scalar_prefetch=1,
            grid=(blocks // PER,),
            in_specs=[whole(*hidden.shape), whole(*weight.shape)]
            + [down_spec(b) for b in range(PER)],
            out_specs=pl.BlockSpec((PER, count, depth), lambda i, order: (i, 0, 0)),
        ),
        compiler_params=pltpu.CompilerParams(
            dimension_semantics=("arbitrary",), vmem_limit_bytes=VMEM
        ),
        cost_estimate=pl.CostEstimate(
            flops=2 * count * both * depth * blocks,
            bytes_accessed=both * depth * blocks * 2,
            transcendentals=0,
        ),
    )(places, hidden, weight, *([down] * PER))


def body(
    mixer_out,
    out_proj,
    residual,
    norm_gain,
    router_weight,
    expert_ids,
    expert_gate,
    expert_up,
    expert_down,
):
    node = lax.axis_index("node")
    local = lax.axis_index("local")
    core = lax.axis_index("tp")
    x, y = local // SIDE, local % SIDE
    half_rows, col_width = residual.shape
    capacity = half_rows // 16
    spots = SIDE * capacity
    part = mixer_out.shape[0] // 2

    gate, up, down = (
        lax.all_gather(w, "tp", axis=0, tiled=True) for w in (expert_gate, expert_up, expert_down)
    )

    first, partner = expert_ids[:, 0], expert_ids[:, 1]
    routed = first < SIDE
    relative = lax.rem(first - node + SIDE, SIDE)
    marks = (routed[:, None] & (relative[:, None] == jnp.arange(SIDE)[None, :])).astype(jnp.int32)
    slots = jnp.sum((jnp.cumsum(marks, axis=0) - marks) * marks, axis=1)
    spot = jnp.where(routed, relative * capacity + slots, -1)
    placed = (spot[:, None] == jnp.arange(spots)[None, :]).astype(BF16)
    picked = spot[None, :] == jnp.arange(spots)[:, None]
    partners = jnp.sum(jnp.where(picked, partner[None, :], 0), axis=1).reshape(SIDE, capacity)
    def to_relative(value):
        value = value.reshape((2, SIDE, 2, part) + value.shape[1:])
        value = jnp.where(x % 2 == 1, value[::-1], value)
        return roll_to(value, y, 1)

    spot_rel = to_relative(spot)
    rest_rel = to_relative(residual)
    mine = [((x + p) % SIDE) // 2 == core for p in range(2)]

    groups = []
    for half, (near, far) in enumerate((("x", "y"), ("y", "x"))):
        own = mixer_out[half * part : (half + 1) * part]
        ahead, across, behind = ring(own, near)
        line = jnp.concatenate([own, ahead] + across + [behind], axis=0)
        groups.append([line] + list(ring(line, far)))

    def project(group):
        pieces = group if isinstance(group, list) else [group]
        dots = [jnp.dot(rows, out_proj, preferred_element_type=F32) for rows in pieces]
        return jnp.concatenate(dots, axis=0).reshape(SIDE, part, col_width)

    results = [[project(group) for group in half] for half in groups]

    def split(blocks, p):
        kept = jnp.where(mine[p], blocks[p], blocks[p + 2])
        sent = jnp.where(mine[p], blocks[p + 2], blocks[p])
        return kept, sent

    streams = {}
    for early in (True, False):
        kept, sent, names = [], [], []
        for at in (0, 1, 3) if early else (2,):
            for p in range(2):
                pair = split(results[0][at], p)
                kept.append(pair[0][None])
                sent.append(pair[1][None])
                names.append((0, at, p))
        pair = split(results[1], 1 if early else 0)
        kept.append(pair[0])
        sent.append(pair[1])
        names += [(1, dy, 1 if early else 0) for dy in range(SIDE)]
        kept = jnp.concatenate(kept, axis=0) + swap_core(jnp.concatenate(sent, axis=0))
        for at, (half, dy, p) in enumerate(names):
            streams[half, dy, p] = rest_rel[p, dy, half].astype(F32) + kept[at]

    bucket = jnp.zeros((spots, col_width), F32)
    for late in (False, True):
        names = [n for n in streams if (n[1] == 2 if n[0] == 0 else n[2] == 0) == late]
        where = jnp.concatenate([spot_rel[p, dy, half] for half, dy, p in names])
        one_hot = (where[None, :] == jnp.arange(spots)[:, None]).astype(BF16)
        rows = jnp.concatenate([streams[n] for n in names], axis=0).astype(BF16)
        bucket += jnp.dot(one_hot, rows, preferred_element_type=F32)
    bucket = bucket.astype(BF16).reshape(SIDE, capacity, col_width)

    stream = jnp.stack(
        [streams[half, dy, p] for p in range(2) for dy in range(SIDE) for half in range(2)]
    ).reshape(2, SIDE, 2, part, col_width)
    stream = roll_to(stream, (SIDE - y) % SIDE, 1)
    stream = jnp.where(x % 2 == 1, stream[::-1], stream).reshape(half_rows, col_width)

    tag = jnp.broadcast_to(partners.astype(BF16)[:, :, None], (SIDE, capacity, 128))
    bucket = jnp.concatenate([bucket, tag], axis=2)
    landed = jnp.concatenate(
        [bucket[0]] + [shift_node(bucket[d], d) for d in (1, 3, 2)], axis=0
    )
    partners = landed[:, col_width].astype(jnp.int32)
    landed = landed[:, :col_width]
    experts = jnp.arange(router_weight.shape[1])[None, :]
    select = (experts == node).astype(F32) - (experts == partners[:, None]).astype(F32)
    got = {(-d) % SIDE: shift_mixed(landed, False, d) for d in (1, 3, 2)}
    line = jnp.stack([landed] + [got[d] for d in range(1, SIDE)], axis=0)
    got = {(-d) % SIDE: shift_mixed(line, True, d) for d in (1, 3, 2)}
    arrived = [line] + [got[d] for d in range(1, SIDE)]
    ring_x = ((x + jnp.arange(SIDE)) % SIDE) * SIDE
    ring_y = (y + jnp.arange(SIDE)) % SIDE

    def places(distance):
        return jnp.where(
            core == 0, ring_x + ring_y[distance], ring_x[distance] + ring_y
        ).astype(jnp.int32)

    carried = None
    for d in (0, 1, 3, 2):
        carried = products(
            arrived[d],
            places(d),
            gate,
            up,
            router_weight.T,
            norm_gain[None, :],
            carried,
            select if d == 2 else None,
        )
    hidden, weight = carried

    terms = {d: down_terms(hidden, weight, places(d), down, col_width) for d in (1, 3, 2, 0)}
    got = [shift_mixed(terms[d], True, d) for d in (1, 3, 2)]
    line = sum((g.astype(F32) for g in got), terms[0].astype(F32)).astype(BF16)
    got = [shift_mixed(line[d], False, d) for d in (1, 3, 2)]
    summed = sum((g.astype(F32) for g in got), line[0].astype(F32)).astype(BF16)
    summed = summed.reshape(SIDE, capacity, col_width)
    back = {d: shift_node(summed[at], -d) for at, d in ((1, 1), (2, 3), (3, 2))}
    returned = jnp.concatenate([summed[0]] + [back[d] for d in range(1, SIDE)], axis=0)
    expert_sum = jnp.dot(placed, returned, preferred_element_type=F32)
    return (stream + expert_sum).astype(BF16)


def solution(mesh):
    placed = (
        P(("node", "local"), "tp"),
        P("tp", "local"),
        P(("node", "tp"), "local"),
        P(),
        P(),
        P(("node", "tp"), None),
        P("node", None, ("local", "tp")),
        P("node", None, ("local", "tp")),
        P("node", ("local", "tp"), None),
    )
    return jax.shard_map(
        body, mesh=mesh, in_specs=placed, out_specs=P(("node", "tp"), "local"), check_vma=False
    )
```

time: 607 us -> 263 us (0.43)
  waiting for transfers between devices: 320 us -> 79.7 us
  local copies, waits for them, and re-layouts: 158 us -> 15.9 us
  Pallas kernels: 0 us -> 53.7 us
  starting transfers between devices: 24.7 us -> 46.9 us
  matrix products: 40.9 us -> 23.4 us
  other arithmetic: 42.9 us -> 27.9 us
    all_to_all x3 -> x0, waiting for transfers between devices: 199 us -> none  [the longest x1 99.1 us: body(): lax.all_to_all(spread, ('node', 'local', 'tp'), split_axis=0, concat_axis...]
    all_gather x1 -> x3, waiting for transfers between devices: 116 us -> 0.01 us  [body(): lax.all_gather(w, 'tp', axis=0, tiled=True)]
    ppermute x0 -> x36, waiting for transfers between devices: none -> 78.3 us  [the longest x16 41.6 us: shift(): return lax.ppermute(value, 'local', pairs)]
    gather x3 -> x0, local copies, waits for them, and re-layouts: 63.8 us -> none  [the longest x2 59.2 us: body(): fetched = returned[flights[None, :], safe_slots]]
    pallas_call x0 -> x8, Pallas kernels: none -> 53.7 us  [the longest x4 32 us: products(): pl.pallas_call(lambda *refs: products_kernel(*refs, first=first, last=las...]
    ppermute x0 -> x36, starting transfers between devices: none -> 46.8 us  [the longest x16 24.2 us: shift(): return lax.ppermute(value, 'local', pairs)]
    unnamed x23 -> x14, local copies, waits for them, and re-layouts: 46.5 us -> 5.01 us
    convert_element_type x2 -> x1, local copies, waits for them, and re-layouts: 29.6 us -> 0.08 us  [body(): partners.astype(BF16)[:, :, None]]
  transfers between devices with their start and end apart: 5 -> 39, of which waited for: 5 -> 17; matrix products, arithmetic and copies ran while one was open for 1% -> 24% of each run, Pallas kernels for 0% -> 18%
where the time goes in v2:
time: 263 us; the launch traced here: 261 us
  waiting for transfers between devices  79.7 us (30%)
  Pallas kernels  53.7 us (20%)
  starting transfers between devices  46.9 us (18%)
  other arithmetic  27.9 us (11%)
  matrix products  23.4 us (9%)
  local copies, waits for them, and re-layouts  15.9 us (6%)
  between operations  13.9 us (5%)
    ppermute x16, waiting for transfers between devices, shift(): return lax.ppermute(value, 'local', pairs)  41.6 us
    pallas_call x4, Pallas kernels, products(): pl.pallas_call(lambda *refs: products_kernel(*refs, first=first, last=las...  32 us
    ppermute x12, waiting for transfers between devices, shift_mixed(): return lax.ppermute(value, ('local', 'tp'), pairs)  29.5 us
    ppermute x16, starting transfers between devices, shift(): return lax.ppermute(value, 'local', pairs)  24.2 us
    pallas_call x4, Pallas kernels, down_terms(): pl.pallas_call(down_kernel, out_shape=jax.ShapeDtypeStruct((blocks, count...  21.7 us
    dot_general x10, matrix products, project(): jnp.dot(rows, out_proj, preferred_element_type=F32)  21.2 us
    ppermute x12, starting transfers between devices, shift_mixed(): return lax.ppermute(value, ('local', 'tp'), pairs)  13.2 us
    unnamed x35, other arithmetic  10.4 us
  transfers between devices with their start and end apart: 39, of which 17 were waited for; matrix products, arithmetic and copies ran while one was open for 24% of the time, Pallas kernels for 18%

profile of v2, /device:TPU:6, one launch (start us, length us, event | category | flops | bytes accessed | tf_op | source)
XLA Modules:
  0.0 261.3 jit_solution(9785293260815954194)
XLA Ops:
  10.6 2.4 collective-permute-start.1
  13.0 3.0 %collective-permute-start.6 = (bf16[64,4096]{1,0:T(8,128)(2,1)S(1)}, bf16[64,4096]{1,0:T(8,128)(2,1)S(1)}, u32[]{:S(2)}, u32[]{:S(2)}) collective-permute-start(bf16[64,4096]{1,0:T(8,128)(2,1)S(1)} %get-tuple-element.38), channel_id=1, source_target_pairs={{0,6},{2,0},{4,2},{6,4},{8,14},{10,8},{12,10},{14,12},{16,22},{18,... | collective-permute-start | bytes 1572872 | tf_op jit(solution)/shard_map/ppermute | solution.py:26
  19.4 4.6 %collective-permute-done.1 = bf16[64,4096]{1,0:T(8,128)(2,1)S(1)} collective-permute-done((bf16[64,4096]{1,0:T(8,128)(2,1)S(1)}, bf16[64,4096]{1,0:T(8,128)(2,1)S(1)}, u32[]{:S(2)}, u32[]{:S(2)}) %collective-permute-start.1) | collective-permute-done | bytes 524320 | tf_op jit(solution)/shard_map/ppermute | solution.py:26
  24.0 3.7 %collective-permute-start.2 = (bf16[32,4096]{1,0:T(8,128)(2,1)S(1)}, bf16[32,4096]{1,0:T(8,128)(2,1)S(1)}, u32[]{:S(2)}, u32[]{:S(2)}) collective-permute-start(bf16[32,4096]{1,0:T(8,128)(2,1)S(1)} %slice.449), channel_id=1, source_target_pairs={{0,8},{2,10},{4,12},{6,14},{8,16},{10,18},{12,20},{14,22},{16,24},... | collective-permute-start | bytes 786440 | tf_op jit(solution)/shard_map/ppermute | solution.py:26
  27.8 2.3 collective-permute-done.7
  30.2 3.3 %collective-permute-start.9 = (bf16[32,4096]{1,0:T(8,128)(2,1)S(1)}, bf16[32,4096]{1,0:T(8,128)(2,1)S(1)}, u32[]{:S(2)}, u32[]{:S(2)}) collective-permute-start(bf16[32,4096]{1,0:T(8,128)(2,1)S(1)} %slice.464), channel_id=1, source_target_pairs={{0,6},{2,0},{4,2},{6,4},{8,14},{10,8},{12,10},{14,12},{16,22},{18,... | collective-permute-start | bytes 786440 | tf_op jit(solution)/shard_map/ppermute | solution.py:26
  38.7 2.0 collective-permute-start.4
  46.8 1.8 broadcast_select_fusion.5.refs_0_.order
  48.6 1.7 broadcast_select_fusion.2.refs_0_.order
  50.2 1.8 broadcast_select_fusion.3.refs_0_.order
  52.2 5.8 %fusion.116 = f32[256,512]{1,0:T(8,128)S(1)} fusion(bf16[256,4096]{1,0:T(8,128)(2,1)} %constant_dynamic-update-slice_fusion, bf16[4096,512]{1,0:T(8,128)(2,1)} %param.10), kind=kOutput, calls=%fused_computation.273 | convolution fusion | flops 1073741824 | bytes 6815744 | tf_op jit(solution)/shard_map/dot_general | solution.py:260
  58.1 25.9 %collective-permute-done.5 = bf16[256,4096]{1,0:T(8,128)(2,1)} collective-permute-done((bf16[256,4096]{1,0:T(8,128)(2,1)}, bf16[256,4096]{1,0:T(8,128)(2,1)}, u32[]{:S(2)}, u32[]{:S(2)}) %collective-permute-start.5) | collective-permute-done | bytes 2097184 | tf_op jit(solution)/shard_map/ppermute | solution.py:26
  84.0 1.6 slice.467
  85.8 1.8 slice.469
  87.5 3.1 %collective-permute-start.14 = (bf16[128,4096]{1,0:T(8,128)(2,1)S(1)}, bf16[128,4096]{1,0:T(8,128)(2,1)S(1)}, u32[]{:S(2)}, u32[]{:S(2)}) collective-permute-start(bf16[128,4096]{1,0:T(8,128)(2,1)S(1)} %slice.469), channel_id=1, source_target_pairs={{0,6},{2,0},{4,2},{6,4},{8,14},{10,8},{12,10},{14,12},{16,22},{18,... | collective-permute-start | bytes 3145736 | tf_op jit(solution)/shard_map/ppermute | solution.py:26
  91.9 1.6 slice.474
  94.7 2.8 %fusion.119 = f32[256,512]{1,0:T(8,128)S(1)} fusion(bf16[256,4096]{1,0:T(8,128)(2,1)} %collective-permute-done.10, bf16[4096,512]{1,0:T(8,128)(2,1)S(1)} %copy-done), kind=kOutput, calls=%fused_computation.276 | convolution fusion | flops 1073741824 | bytes 6815744 | tf_op jit(solution)/shard_map/dot_general | solution.py:260
  97.5 2.8 %fusion.117 = f32[256,512]{1,0:T(8,128)S(1)} fusion(bf16[256,4096]{1,0:T(8,128)(2,1)} %collective-permute-done.4, bf16[4096,512]{1,0:T(8,128)(2,1)S(1)} %copy-done), kind=kOutput, calls=%fused_computation.274 | convolution fusion | flops 1073741824 | bytes 6815744 | tf_op jit(solution)/shard_map/dot_general | solution.py:260
  100.4 2.8 %fusion.118 = f32[256,512]{1,0:T(8,128)S(1)} fusion(bf16[256,4096]{1,0:T(8,128)(2,1)} %collective-permute-done.5, bf16[4096,512]{1,0:T(8,128)(2,1)S(1)} %copy-done), kind=kOutput, calls=%fused_computation.275 | convolution fusion | flops 1073741824 | bytes 6815744 | tf_op jit(solution)/shard_map/dot_general | solution.py:260
  104.7 3.7 %collective-permute-done.13 = bf16[128,4096]{1,0:T(8,128)(2,1)S(1)} collective-permute-done((bf16[128,4096]{1,0:T(8,128)(2,1)S(1)}, bf16[128,4096]{1,0:T(8,128)(2,1)S(1)}, u32[]{:S(2)}, u32[]{:S(2)}) %collective-permute-start.13) | collective-permute-done | bytes 1048608 | tf_op jit(solution)/shard_map/ppermute | solution.py:26
  110.2 1.6 collective-permute-done.15
  112.5 3.2 %collective-permute-done.16 = bf16[128,4096]{1,0:T(8,128)(2,1)S(1)} collective-permute-done((bf16[128,4096]{1,0:T(8,128)(2,1)S(1)}, bf16[128,4096]{1,0:T(8,128)(2,1)S(1)}, u32[]{:S(2)}, u32[]{:S(2)}) %collective-permute-start.16) | collective-permute-done | bytes 1048608 | tf_op jit(solution)/shard_map/ppermute | solution.py:26
  116.5 2.8 %fusion.10 = (f32[256,512]{1,0:T(8,128)S(1)}, f32[256,512]{1,0:T(8,128)S(1)}) fusion(f32[128,512]{1,0:T(8,128)S(1)} %fusion.123, f32[128,512]{1,0:T(8,128)S(1)} %fusion.122, pred[]{:T(512)S(6)} %eq.141, bf16[256,4096]{1,0:T(8,128)(2,1)} %constant_dynamic-update-slice_fusion.5, bf16[4096,512]{1,0:T(8,128)(2,1)S(1)} %copy-done), kind=kOutput, calls=%fused_computation.31 | convolution fusion | flops 1074135040 | bytes 7864321 | tf_op jit(solution)/shard_map/dot_general | solution.py:260
  119.5 1.8 broadcast_select_fusion.4.refs_0_.order
  124.1 2.0 collective-permute-start.18
  126.2 2.1 collective-permute-start.19
  128.3 1.9 collective-permute-start.20
  135.5 2.2 collective-permute-start.23
  139.1 5.8 %collective-permute-done.21 = bf16[256,512]{1,0:T(8,128)(2,1)S(1)} collective-permute-done((bf16[256,512]{1,0:T(8,128)(2,1)S(1)}, bf16[256,512]{1,0:T(8,128)(2,1)S(1)}, u32[]{:S(2)}, u32[]{:S(2)}) %collective-permute-start.21) | collective-permute-done | bytes 262176 | tf_op jit(solution)/shard_map/ppermute | solution.py:37
  152.4 7.5 %shard_map.91 = (f32[4,256,384]{2,1,0:T(8,128)}, f32[256,16]{1,0:T(8,128)}, f32[256,128]{1,0:T(8,128)}) custom-call(s32[4]{0:T(128)} %broadcast_select_fusion.5.refs_0_.order, bf16[4,256,512]{2,1,0:T(8,128)(2,1)} %pad_maximum_fusion.refs_1_, bf16[2,8192,384]{2,1,0:T(8,128)(2,1)} %all-gather.4.cloned.1.call-done.refs_2_, ...), custom_call_target="tpu_custom_call" | custom-call | flops 1610612736 | bytes 6291456 | tf_op jit(solution)/shard_map/pallas_call | solution.py:148
  160.0 2.0 collective-permute-done.26.refs_1_
  162.0 8.1 %shard_map.92 = (f32[4,256,384]{2,1,0:T(8,128)}, f32[256,16]{1,0:T(8,128)}, f32[256,128]{1,0:T(8,128)}) custom-call(s32[4]{0:T(128)} %broadcast_select_fusion.2.refs_0_.order, bf16[4,256,512]{2,1,0:T(8,128)(2,1)} %collective-permute-done.26.refs_1_, bf16[2,8192,384]{2,1,0:T(8,128)(2,1)} %all-gather.4.cloned.1.call-done.refs_2_, ...), custom_call_target="tpu_custom_call" | custom-call | flops 1610612736 | bytes 6291456 | tf_op jit(solution)/shard_map/pallas_call | solution.py:148
  170.1 4.9 %collective-permute-done.25.refs_1_ = bf16[4,256,512]{2,1,0:T(8,128)(2,1)} collective-permute-done((bf16[4,256,512]{2,1,0:T(8,128)(2,1)}, bf16[4,256,512]{2,1,0:T(8,128)(2,1)}, u32[]{:S(2)}, u32[]{:S(2)}) %collective-permute-start.25) | collective-permute-done | bytes 1048608 | tf_op jit(solution)/shard_map/ppermute | solution.py:37
  175.0 8.2 %shard_map.93 = (f32[4,256,384]{2,1,0:T(8,128)}, f32[256,16]{1,0:T(8,128)}, f32[256,128]{1,0:T(8,128)}) custom-call(s32[4]{0:T(128)} %broadcast_select_fusion.3.refs_0_.order, bf16[4,256,512]{2,1,0:T(8,128)(2,1)} %collective-permute-done.25.refs_1_, bf16[2,8192,384]{2,1,0:T(8,128)(2,1)} %all-gather.4.cloned.1.call-done.refs_2_, ...), custom_call_target="tpu_custom_call" | custom-call | flops 1610612736 | bytes 6291456 | tf_op jit(solution)/shard_map/pallas_call | solution.py:148
  183.2 8.2 %shard_map.94 = (bf16[256,768]{1,0:T(8,128)(2,1)}, f32[256,128]{1,0:T(8,128)}) custom-call(s32[4]{0:T(128)} %broadcast_select_fusion.4.refs_0_.order, bf16[4,256,512]{2,1,0:T(8,128)(2,1)} %collective-permute-done.24.refs_1_, bf16[2,8192,384]{2,1,0:T(8,128)(2,1)} %all-gather.4.cloned.1.call-done.refs_2_, ...), custom_call_target="tpu_custom_call" | custom-call | flops 1610612736 | bytes 6291456 | tf_op jit(solution)/shard_map/pallas_call | solution.py:148
  191.4 5.4 %shard_map.96 = bf16[4,256,512]{2,1,0:T(8,128)(2,1)} custom-call(s32[4]{0:T(128)} %broadcast_select_fusion.2.refs_0_.order, bf16[256,768]{1,0:T(8,128)(2,1)} %get-tuple-element.25.hidden, f32[256,128]{1,0:T(8,128)} %get-tuple-element.26.weight, bf16[2,384,8192]{2,1,0:T(8,128)(2,1)} %all-gather.8.cloned.1.call-done.refs_0_), custom_call_target="tpu_custom_call" | custom-call | flops 805306368 | bytes 3145728 | tf_op jit(solution)/shard_map/pallas_call | solution.py:188
  196.8 5.4 %shard_map.97 = bf16[4,256,512]{2,1,0:T(8,128)(2,1)} custom-call(s32[4]{0:T(128)} %broadcast_select_fusion.3.refs_0_.order, bf16[256,768]{1,0:T(8,128)(2,1)} %get-tuple-element.25.hidden, f32[256,128]{1,0:T(8,128)} %get-tuple-element.26.weight, bf16[2,384,8192]{2,1,0:T(8,128)(2,1)} %all-gather.8.cloned.1.call-done.refs_0_), custom_call_target="tpu_custom_call" | custom-call | flops 805306368 | bytes 3145728 | tf_op jit(solution)/shard_map/pallas_call | solution.py:188
  202.3 3.2 %collective-permute-start.28 = (bf16[4,256,512]{2,1,0:T(8,128)(2,1)}, bf16[4,256,512]{2,1,0:T(8,128)(2,1)S(1)}, u32[]{:S(2)}, u32[]{:S(2)}) collective-permute-start(bf16[4,256,512]{2,1,0:T(8,128)(2,1)} %shard_map.97), channel_id=1, source_target_pairs={{0,6},{1,25},{2,0},{3,27},{4,2},{5,29},{6,4},{7,31},{8,14},{9,1},{... | collective-permute-start | bytes 3145736 | tf_op jit(solution)/shard_map/ppermute | solution.py:37
  205.5 5.4 %shard_map.98 = bf16[4,256,512]{2,1,0:T(8,128)(2,1)} custom-call(s32[4]{0:T(128)} %broadcast_select_fusion.4.refs_0_.order, bf16[256,768]{1,0:T(8,128)(2,1)} %get-tuple-element.25.hidden, f32[256,128]{1,0:T(8,128)} %get-tuple-element.26.weight, bf16[2,384,8192]{2,1,0:T(8,128)(2,1)} %all-gather.8.cloned.1.call-done.refs_0_), custom_call_target="tpu_custom_call" | custom-call | flops 805306368 | bytes 3145728 | tf_op jit(solution)/shard_map/pallas_call | solution.py:188
  214.2 5.4 %shard_map.95 = bf16[4,256,512]{2,1,0:T(8,128)(2,1)} custom-call(s32[4]{0:T(128)} %broadcast_select_fusion.5.refs_0_.order, bf16[256,768]{1,0:T(8,128)(2,1)} %get-tuple-element.25.hidden, f32[256,128]{1,0:T(8,128)} %get-tuple-element.26.weight, bf16[2,384,8192]{2,1,0:T(8,128)(2,1)} %all-gather.8.cloned.1.call-done.refs_0_), custom_call_target="tpu_custom_call" | custom-call | flops 805306368 | bytes 3145728 | tf_op jit(solution)/shard_map/pallas_call | solution.py:188
  219.6 9.7 %collective-permute-done.28 = bf16[4,256,512]{2,1,0:T(8,128)(2,1)S(1)} collective-permute-done((bf16[4,256,512]{2,1,0:T(8,128)(2,1)}, bf16[4,256,512]{2,1,0:T(8,128)(2,1)S(1)}, u32[]{:S(2)}, u32[]{:S(2)}) %collective-permute-start.28) | collective-permute-done | bytes 1048608 | tf_op jit(solution)/shard_map/ppermute | solution.py:37
  229.4 1.8 add_convert_fusion
  231.2 2.4 collective-permute-start.30
  235.8 2.1 fusion
  238.0 6.1 %collective-permute-done.31 = bf16[256,512]{1,0:T(8,128)(2,1)S(1)} collective-permute-done((bf16[256,512]{1,0:T(8,128)(2,1)S(1)}, bf16[256,512]{1,0:T(8,128)(2,1)S(1)}, u32[]{:S(2)}, u32[]{:S(2)}) %collective-permute-start.31) | collective-permute-done | bytes 262176 | tf_op jit(solution)/shard_map/ppermute | solution.py:37
  244.2 1.9 collective-permute-start.33
  247.6 1.6 collective-permute-done.33
  249.2 3.2 %collective-permute-done.34 = bf16[64,512]{1,0:T(8,128)(2,1)S(1)} collective-permute-done((bf16[64,512]{1,0:T(8,128)(2,1)S(1)}, bf16[64,512]{1,0:T(8,128)(2,1)S(1)}, u32[]{:S(2)}, u32[]{:S(2)}) %collective-permute-start.34) | collective-permute-done | bytes 65568 | tf_op jit(solution)/shard_map/ppermute | solution.py:16
  (169 shorter events, 52.6 us)
Async XLA Ops:
  6.5 145.9 %all-gather.4.cloned.1.call-start = ((), (), s32[]{:S(2)}) async-start(), calls=%async_computation | async-start | bytes 18874368 | tf_op jit(solution)/shard_map/all_gather | solution.py:230
  7.3 1.2 copy-start.1
  7.3 145.2 %all-gather.6.cloned.1.call-start = ((), (), s32[]{:S(2)}) async-start(), calls=%async_computation.1 | async-start | bytes 18874368 | tf_op jit(solution)/shard_map/all_gather | solution.py:230
  8.0 183.4 %all-gather.8.cloned.1.call-start = ((), (), s32[]{:S(2)}) async-start(), calls=%async_computation.2 | async-start | bytes 18874368 | tf_op jit(solution)/shard_map/all_gather | solution.py:230
  9.8 17.9 %collective-permute-start = (bf16[64,4096]{1,0:T(8,128)(2,1)S(1)}, bf16[64,4096]{1,0:T(8,128)(2,1)S(1)}, u32[]{:S(2)}, u32[]{:S(2)}) collective-permute-start(bf16[64,4096]{1,0:T(8,128)(2,1)S(1)} %get-tuple-element.41), channel_id=1, source_target_pairs={{0,24},{2,26},{4,28},{6,30},{8,0},{10,2},{12,4},{14,6},{16,8},{18,... | collective-permute-start | bytes 1572872 | tf_op jit(solution)/shard_map/ppermute | solution.py:26
  10.6 13.4 %collective-permute-start.1 = (bf16[64,4096]{1,0:T(8,128)(2,1)S(1)}, bf16[64,4096]{1,0:T(8,128)(2,1)S(1)}, u32[]{:S(2)}, u32[]{:S(2)}) collective-permute-start(bf16[64,4096]{1,0:T(8,128)(2,1)S(1)} %get-tuple-element.41), channel_id=1, source_target_pairs={{0,8},{2,10},{4,12},{6,14},{8,16},{10,18},{12,20},{14,22},{16,24},... | collective-permute-start | bytes 1572872 | tf_op jit(solution)/shard_map/ppermute | solution.py:26
  13.0 3.2 %copy-start.3 = (s32[1024,2]{0,1:T(2,128)S(1)}, s32[1024,2]{0,1:T(2,128)}, u32[]{:S(2)}) copy-start(s32[1024,2]{0,1:T(2,128)} %param.14) | copy-start | bytes 24580
  13.0 17.2 %collective-permute-start.6 = (bf16[64,4096]{1,0:T(8,128)(2,1)S(1)}, bf16[64,4096]{1,0:T(8,128)(2,1)S(1)}, u32[]{:S(2)}, u32[]{:S(2)}) collective-permute-start(bf16[64,4096]{1,0:T(8,128)(2,1)S(1)} %get-tuple-element.38), channel_id=1, source_target_pairs={{0,6},{2,0},{4,2},{6,4},{8,14},{10,8},{12,10},{14,12},{16,22},{18,... | collective-permute-start | bytes 1572872 | tf_op jit(solution)/shard_map/ppermute | solution.py:26
  16.0 14.0 %collective-permute-start.7 = (bf16[64,4096]{1,0:T(8,128)(2,1)S(1)}, bf16[64,4096]{1,0:T(8,128)(2,1)S(1)}, u32[]{:S(2)}, u32[]{:S(2)}) collective-permute-start(bf16[64,4096]{1,0:T(8,128)(2,1)S(1)} %get-tuple-element.38), channel_id=1, source_target_pairs={{0,2},{2,4},{4,6},{6,0},{8,10},{10,12},{12,14},{14,8},{16,18},{18,... | collective-permute-start | bytes 1572872 | tf_op jit(solution)/shard_map/ppermute | solution.py:26
  24.0 11.2 %collective-permute-start.2 = (bf16[32,4096]{1,0:T(8,128)(2,1)S(1)}, bf16[32,4096]{1,0:T(8,128)(2,1)S(1)}, u32[]{:S(2)}, u32[]{:S(2)}) collective-permute-start(bf16[32,4096]{1,0:T(8,128)(2,1)S(1)} %slice.449), channel_id=1, source_target_pairs={{0,8},{2,10},{4,12},{6,14},{8,16},{10,18},{12,20},{14,22},{16,24},... | collective-permute-start | bytes 786440 | tf_op jit(solution)/shard_map/ppermute | solution.py:26
  27.7 8.2 %collective-permute-start.3 = (bf16[32,4096]{1,0:T(8,128)(2,1)S(1)}, bf16[32,4096]{1,0:T(8,128)(2,1)S(1)}, u32[]{:S(2)}, u32[]{:S(2)}) collective-permute-start(bf16[32,4096]{1,0:T(8,128)(2,1)S(1)} %slice.450), channel_id=1, source_target_pairs={{0,24},{2,26},{4,28},{6,30},{8,0},{10,2},{12,4},{14,6},{16,8},{18,... | collective-permute-start | bytes 786440 | tf_op jit(solution)/shard_map/ppermute | solution.py:26
  30.1 10.6 %collective-permute-start.8 = (bf16[32,4096]{1,0:T(8,128)(2,1)S(1)}, bf16[32,4096]{1,0:T(8,128)(2,1)S(1)}, u32[]{:S(2)}, u32[]{:S(2)}) collective-permute-start(bf16[32,4096]{1,0:T(8,128)(2,1)S(1)} %slice.463), channel_id=1, source_target_pairs={{0,2},{2,4},{4,6},{6,0},{8,10},{10,12},{12,14},{14,8},{16,18},{18,... | collective-permute-start | bytes 786440 | tf_op jit(solution)/shard_map/ppermute | solution.py:26
  30.2 11.2 %collective-permute-start.9 = (bf16[32,4096]{1,0:T(8,128)(2,1)S(1)}, bf16[32,4096]{1,0:T(8,128)(2,1)S(1)}, u32[]{:S(2)}, u32[]{:S(2)}) collective-permute-start(bf16[32,4096]{1,0:T(8,128)(2,1)S(1)} %slice.464), channel_id=1, source_target_pairs={{0,6},{2,0},{4,2},{6,4},{8,14},{10,8},{12,10},{14,12},{16,22},{18,... | collective-permute-start | bytes 786440 | tf_op jit(solution)/shard_map/ppermute | solution.py:26
  35.2 16.8 %copy-start.2 = (bf16[1024,512]{1,0:T(8,128)(2,1)S(1)}, bf16[1024,512]{1,0:T(8,128)(2,1)}, u32[]{:S(2)}) copy-start(bf16[1024,512]{1,0:T(8,128)(2,1)} %param.11) | copy-start | bytes 3145732
  37.5 46.6 %collective-permute-start.5 = (bf16[256,4096]{1,0:T(8,128)(2,1)}, bf16[256,4096]{1,0:T(8,128)(2,1)}, u32[]{:S(2)}, u32[]{:S(2)}) collective-permute-start(bf16[256,4096]{1,0:T(8,128)(2,1)} %constant_dynamic-update-slice_fusion), channel_id=1, source_target_pairs={{0,2},{2,4},{4,6},{6,0},{8,10},{10,12},{12,14},{14,8},{16,18},{18,... | collective-permute-start | bytes 6291464 | tf_op jit(solution)/shard_map/ppermute | solution.py:26
  38.7 47.0 %collective-permute-start.4 = (bf16[256,4096]{1,0:T(8,128)(2,1)}, bf16[256,4096]{1,0:T(8,128)(2,1)}, u32[]{:S(2)}, u32[]{:S(2)}) collective-permute-start(bf16[256,4096]{1,0:T(8,128)(2,1)} %constant_dynamic-update-slice_fusion), channel_id=1, source_target_pairs={{0,6},{2,0},{4,2},{6,4},{8,14},{10,8},{12,10},{14,12},{16,22},{18,... | collective-permute-start | bytes 6291464 | tf_op jit(solution)/shard_map/ppermute | solution.py:26
  43.0 47.7 %collective-permute-start.11 = (bf16[256,4096]{1,0:T(8,128)(2,1)}, bf16[256,4096]{1,0:T(8,128)(2,1)S(1)}, u32[]{:S(2)}, u32[]{:S(2)}) collective-permute-start(bf16[256,4096]{1,0:T(8,128)(2,1)} %constant_dynamic-update-slice_fusion.5), channel_id=1, source_target_pairs={{0,8},{2,10},{4,12},{6,14},{8,16},{10,18},{12,20},{14,22},{16,24},... | collective-permute-start | bytes 6291464 | tf_op jit(solution)/shard_map/ppermute | solution.py:26
  43.9 48.0 %collective-permute-start.10 = (bf16[256,4096]{1,0:T(8,128)(2,1)}, bf16[256,4096]{1,0:T(8,128)(2,1)}, u32[]{:S(2)}, u32[]{:S(2)}) collective-permute-start(bf16[256,4096]{1,0:T(8,128)(2,1)} %constant_dynamic-update-slice_fusion.5), channel_id=1, source_target_pairs={{0,24},{2,26},{4,28},{6,30},{8,0},{10,2},{12,4},{14,6},{16,8},{18,... | collective-permute-start | bytes 6291464 | tf_op jit(solution)/shard_map/ppermute | solution.py:26
  85.6 22.8 %collective-permute-start.13 = (bf16[128,4096]{1,0:T(8,128)(2,1)S(1)}, bf16[128,4096]{1,0:T(8,128)(2,1)S(1)}, u32[]{:S(2)}, u32[]{:S(2)}) collective-permute-start(bf16[128,4096]{1,0:T(8,128)(2,1)S(1)} %slice.467), channel_id=1, source_target_pairs={{0,2},{2,4},{4,6},{6,0},{8,10},{10,12},{12,14},{14,8},{16,18},{18,... | collective-permute-start | bytes 3145736 | tf_op jit(solution)/shard_map/ppermute | solution.py:26
  85.7 9.0 %copy-start = (bf16[4096,512]{1,0:T(8,128)(2,1)S(1)}, bf16[4096,512]{1,0:T(8,128)(2,1)}, u32[]{:S(2)}) copy-start(bf16[4096,512]{1,0:T(8,128)(2,1)} %param.10) | copy-start | bytes 12582916
  87.5 22.0 %collective-permute-start.14 = (bf16[128,4096]{1,0:T(8,128)(2,1)S(1)}, bf16[128,4096]{1,0:T(8,128)(2,1)S(1)}, u32[]{:S(2)}, u32[]{:S(2)}) collective-permute-start(bf16[128,4096]{1,0:T(8,128)(2,1)S(1)} %slice.469), channel_id=1, source_target_pairs={{0,6},{2,0},{4,2},{6,4},{8,14},{10,8},{12,10},{14,12},{16,22},{18,... | collective-permute-start | bytes 3145736 | tf_op jit(solution)/shard_map/ppermute | solution.py:26
  90.7 21.1 %collective-permute-start.15 = (bf16[128,4096]{1,0:T(8,128)(2,1)S(1)}, bf16[128,4096]{1,0:T(8,128)(2,1)S(1)}, u32[]{:S(2)}, u32[]{:S(2)}) collective-permute-start(bf16[128,4096]{1,0:T(8,128)(2,1)S(1)} %slice.473), channel_id=1, source_target_pairs={{0,8},{2,10},{4,12},{6,14},{8,16},{10,18},{12,20},{14,22},{16,24},... | collective-permute-start | bytes 3145736 | tf_op jit(solution)/shard_map/ppermute | solution.py:26
  93.5 22.2 %collective-permute-start.16 = (bf16[128,4096]{1,0:T(8,128)(2,1)S(1)}, bf16[128,4096]{1,0:T(8,128)(2,1)S(1)}, u32[]{:S(2)}, u32[]{:S(2)}) collective-permute-start(bf16[128,4096]{1,0:T(8,128)(2,1)S(1)} %slice.474), channel_id=1, source_target_pairs={{0,24},{2,26},{4,28},{6,30},{8,0},{10,2},{12,4},{14,6},{16,8},{18,... | collective-permute-start | bytes 3145736 | tf_op jit(solution)/shard_map/ppermute | solution.py:26
  104.6 17.1 %collective-permute-start.12 = (f32[10,64,512]{2,1,0:T(8,128)S(1)}, f32[10,64,512]{2,1,0:T(8,128)S(1)}, u32[]{:S(2)}, u32[]{:S(2)}) collective-permute-start(f32[10,64,512]{2,1,0:T(8,128)S(1)} %constant_dynamic-update-slice_fusion.11), channel_id=1, source_target_pairs={{0,1},{1,0},{2,3},{3,2},{4,5},{5,4},{6,7},{7,6},{8,9},{9,8},{10,11... | collective-permute-start | bytes 3932168 | tf_op jit(solution)/shard_map/ppermute | solution.py:41
  119.4 3.3 %collective-permute-start.17 = (f32[6,64,512]{2,1,0:T(8,128)S(1)}, f32[6,64,512]{2,1,0:T(8,128)S(1)}, u32[]{:S(2)}, u32[]{:S(2)}) collective-permute-start(f32[6,64,512]{2,1,0:T(8,128)S(1)} %pad_maximum_fusion.1), channel_id=1, source_target_pairs={{0,1},{1,0},{2,3},{3,2},{4,5},{5,4},{6,7},{7,6},{8,9},{9,8},{10,11... | collective-permute-start | bytes 2359304 | tf_op jit(solution)/shard_map/ppermute | solution.py:41
  124.1 8.7 %collective-permute-start.18 = (bf16[64,640]{1,0:T(8,128)(2,1)S(1)}, bf16[64,640]{1,0:T(8,128)(2,1)S(1)}, u32[]{:S(2)}, u32[]{:S(2)}) collective-permute-start(bf16[64,640]{1,0:T(8,128)(2,1)S(1)} %get-tuple-element.61), channel_id=1, source_target_pairs={{0,32},{32,64},{64,96},{96,0},{1,33},{33,65},{65,97},{97,1},{2,34}... | collective-permute-start | bytes 245768 | tf_op jit(solution)/shard_map/ppermute | solution.py:16
  126.2 6.7 %collective-permute-start.19 = (bf16[64,640]{1,0:T(8,128)(2,1)S(1)}, bf16[64,640]{1,0:T(8,128)(2,1)S(1)}, u32[]{:S(2)}, u32[]{:S(2)}) collective-permute-start(bf16[64,640]{1,0:T(8,128)(2,1)S(1)} %get-tuple-element.63), channel_id=1, source_target_pairs={{0,96},{32,0},{64,32},{96,64},{1,97},{33,1},{65,33},{97,65},{2,98}... | collective-permute-start | bytes 245768 | tf_op jit(solution)/shard_map/ppermute | solution.py:16
  128.3 6.1 %collective-permute-start.20 = (bf16[64,640]{1,0:T(8,128)(2,1)S(1)}, bf16[64,640]{1,0:T(8,128)(2,1)S(1)}, u32[]{:S(2)}, u32[]{:S(2)}) collective-permute-start(bf16[64,640]{1,0:T(8,128)(2,1)S(1)} %get-tuple-element.62), channel_id=1, source_target_pairs={{0,64},{32,96},{64,0},{96,32},{1,65},{33,97},{65,1},{97,33},{2,66}... | collective-permute-start | bytes 245768 | tf_op jit(solution)/shard_map/ppermute | solution.py:16
  134.4 10.5 %collective-permute-start.21 = (bf16[256,512]{1,0:T(8,128)(2,1)S(1)}, bf16[256,512]{1,0:T(8,128)(2,1)S(1)}, u32[]{:S(2)}, u32[]{:S(2)}) collective-permute-start(bf16[256,512]{1,0:T(8,128)(2,1)S(1)} %get-tuple-element.59), channel_id=1, source_target_pairs={{0,24},{1,7},{2,26},{3,1},{4,28},{5,3},{6,30},{7,5},{8,0},{9,15},{... | collective-permute-start | bytes 786440 | tf_op jit(solution)/shard_map/ppermute | solution.py:37
  134.5 10.4 %collective-permute-start.22 = (bf16[256,512]{1,0:T(8,128)(2,1)S(1)}, bf16[256,512]{1,0:T(8,128)(2,1)S(1)}, u32[]{:S(2)}, u32[]{:S(2)}) collective-permute-start(bf16[256,512]{1,0:T(8,128)(2,1)S(1)} %get-tuple-element.59), channel_id=1, source_target_pairs={{0,16},{1,5},{2,18},{3,7},{4,20},{5,1},{6,22},{7,3},{8,24},{9,13},... | collective-permute-start | bytes 786440 | tf_op jit(solution)/shard_map/ppermute | solution.py:37
  135.5 10.3 %collective-permute-start.23 = (bf16[256,512]{1,0:T(8,128)(2,1)S(1)}, bf16[256,512]{1,0:T(8,128)(2,1)S(1)}, u32[]{:S(2)}, u32[]{:S(2)}) collective-permute-start(bf16[256,512]{1,0:T(8,128)(2,1)S(1)} %get-tuple-element.59), channel_id=1, source_target_pairs={{0,8},{1,3},{2,10},{3,5},{4,12},{5,7},{6,14},{7,1},{8,16},{9,11},{... | collective-permute-start | bytes 786440 | tf_op jit(solution)/shard_map/ppermute | solution.py:37
  146.9 15.1 %collective-permute-start.26 = (bf16[4,256,512]{2,1,0:T(8,128)(2,1)}, bf16[4,256,512]{2,1,0:T(8,128)(2,1)}, u32[]{:S(2)}, u32[]{:S(2)}) collective-permute-start(bf16[4,256,512]{2,1,0:T(8,128)(2,1)} %pad_maximum_fusion.refs_1_), channel_id=1, source_target_pairs={{0,6},{1,25},{2,0},{3,27},{4,2},{5,29},{6,4},{7,31},{8,14},{9,1},{... | collective-permute-start | bytes 3145736 | tf_op jit(solution)/shard_map/ppermute | solution.py:37
  147.5 27.6 %collective-permute-start.25 = (bf16[4,256,512]{2,1,0:T(8,128)(2,1)}, bf16[4,256,512]{2,1,0:T(8,128)(2,1)}, u32[]{:S(2)}, u32[]{:S(2)}) collective-permute-start(bf16[4,256,512]{2,1,0:T(8,128)(2,1)} %pad_maximum_fusion.refs_1_), channel_id=1, source_target_pairs={{0,2},{1,9},{2,4},{3,11},{4,6},{5,13},{6,0},{7,15},{8,10},{9,17},{... | collective-permute-start | bytes 3145736 | tf_op jit(solution)/shard_map/ppermute | solution.py:37
  149.6 33.6 %collective-permute-start.24 = (bf16[4,256,512]{2,1,0:T(8,128)(2,1)}, bf16[4,256,512]{2,1,0:T(8,128)(2,1)}, u32[]{:S(2)}, u32[]{:S(2)}) collective-permute-start(bf16[4,256,512]{2,1,0:T(8,128)(2,1)} %pad_maximum_fusion.refs_1_), channel_id=1, source_target_pairs={{0,4},{1,17},{2,6},{3,19},{4,0},{5,21},{6,2},{7,23},{8,12},{9,25},... | collective-permute-start | bytes 3145736 | tf_op jit(solution)/shard_map/ppermute | solution.py:37
  196.8 22.8 %collective-permute-start.27 = (bf16[4,256,512]{2,1,0:T(8,128)(2,1)}, bf16[4,256,512]{2,1,0:T(8,128)(2,1)S(1)}, u32[]{:S(2)}, u32[]{:S(2)}) collective-permute-start(bf16[4,256,512]{2,1,0:T(8,128)(2,1)} %shard_map.96), channel_id=1, source_target_pairs={{0,2},{1,9},{2,4},{3,11},{4,6},{5,13},{6,0},{7,15},{8,10},{9,17},{... | collective-permute-start | bytes 3145736 | tf_op jit(solution)/shard_map/ppermute | solution.py:37
  202.3 27.1 %collective-permute-start.28 = (bf16[4,256,512]{2,1,0:T(8,128)(2,1)}, bf16[4,256,512]{2,1,0:T(8,128)(2,1)S(1)}, u32[]{:S(2)}, u32[]{:S(2)}) collective-permute-start(bf16[4,256,512]{2,1,0:T(8,128)(2,1)} %shard_map.97), channel_id=1, source_target_pairs={{0,6},{1,25},{2,0},{3,27},{4,2},{5,29},{6,4},{7,31},{8,14},{9,1},{... | collective-permute-start | bytes 3145736 | tf_op jit(solution)/shard_map/ppermute | solution.py:37
  210.9 18.5 %collective-permute-start.29 = (bf16[4,256,512]{2,1,0:T(8,128)(2,1)}, bf16[4,256,512]{2,1,0:T(8,128)(2,1)S(1)}, u32[]{:S(2)}, u32[]{:S(2)}) collective-permute-start(bf16[4,256,512]{2,1,0:T(8,128)(2,1)} %shard_map.98), channel_id=1, source_target_pairs={{0,4},{1,17},{2,6},{3,19},{4,0},{5,21},{6,2},{7,23},{8,12},{9,25},... | collective-permute-start | bytes 3145736 | tf_op jit(solution)/shard_map/ppermute | solution.py:37
  231.2 6.7 %collective-permute-start.30 = (bf16[256,512]{1,0:T(8,128)(2,1)S(1)}, bf16[256,512]{1,0:T(8,128)(2,1)S(1)}, u32[]{:S(2)}, u32[]{:S(2)}) collective-permute-start(bf16[256,512]{1,0:T(8,128)(2,1)S(1)} %get-tuple-element.29), channel_id=1, source_target_pairs={{0,8},{1,3},{2,10},{3,5},{4,12},{5,7},{6,14},{7,1},{8,16},{9,11},{... | collective-permute-start | bytes 786440 | tf_op jit(solution)/shard_map/ppermute | solution.py:37
  233.6 10.4 %collective-permute-start.31 = (bf16[256,512]{1,0:T(8,128)(2,1)S(1)}, bf16[256,512]{1,0:T(8,128)(2,1)S(1)}, u32[]{:S(2)}, u32[]{:S(2)}) collective-permute-start(bf16[256,512]{1,0:T(8,128)(2,1)S(1)} %get-tuple-element.31), channel_id=1, source_target_pairs={{0,24},{1,7},{2,26},{3,1},{4,28},{5,3},{6,30},{7,5},{8,0},{9,15},{... | collective-permute-start | bytes 786440 | tf_op jit(solution)/shard_map/ppermute | solution.py:37
  233.6 10.4 %collective-permute-start.32 = (bf16[256,512]{1,0:T(8,128)(2,1)S(1)}, bf16[256,512]{1,0:T(8,128)(2,1)S(1)}, u32[]{:S(2)}, u32[]{:S(2)}) collective-permute-start(bf16[256,512]{1,0:T(8,128)(2,1)S(1)} %get-tuple-element.30), channel_id=1, source_target_pairs={{0,16},{1,5},{2,18},{3,7},{4,20},{5,1},{6,22},{7,3},{8,24},{9,13},... | collective-permute-start | bytes 786440 | tf_op jit(solution)/shard_map/ppermute | solution.py:37
  244.2 5.0 %collective-permute-start.33 = (bf16[64,512]{1,0:T(8,128)(2,1)S(1)}, bf16[64,512]{1,0:T(8,128)(2,1)S(1)}, u32[]{:S(2)}, u32[]{:S(2)}) collective-permute-start(bf16[64,512]{1,0:T(8,128)(2,1)S(1)} %get-tuple-element.67), channel_id=1, source_target_pairs={{0,96},{32,0},{64,32},{96,64},{1,97},{33,1},{65,33},{97,65},{2,98}... | collective-permute-start | bytes 196616 | tf_op jit(solution)/shard_map/ppermute | solution.py:16
  246.1 6.4 %collective-permute-start.34 = (bf16[64,512]{1,0:T(8,128)(2,1)S(1)}, bf16[64,512]{1,0:T(8,128)(2,1)S(1)}, u32[]{:S(2)}, u32[]{:S(2)}) collective-permute-start(bf16[64,512]{1,0:T(8,128)(2,1)S(1)} %get-tuple-element.66), channel_id=1, source_target_pairs={{0,64},{32,96},{64,0},{96,32},{1,65},{33,97},{65,1},{97,33},{2,66}... | collective-permute-start | bytes 196616 | tf_op jit(solution)/shard_map/ppermute | solution.py:16
  247.4 6.0 %collective-permute-start.35 = (bf16[64,512]{1,0:T(8,128)(2,1)S(1)}, bf16[64,512]{1,0:T(8,128)(2,1)S(1)}, u32[]{:S(2)}, u32[]{:S(2)}) collective-permute-start(bf16[64,512]{1,0:T(8,128)(2,1)S(1)} %get-tuple-element.65), channel_id=1, source_target_pairs={{0,32},{32,64},{64,96},{96,0},{1,33},{33,65},{65,97},{97,1},{2,34}... | collective-permute-start | bytes 196616 | tf_op jit(solution)/shard_map/ppermute | solution.py:16
Sparse Core Ops, SparseCore 0:
  9.0 30.0 all-gather.3
  40.8 28.8 all-gather.5
  71.4 28.9 all-gather.7
